TPU v7x, 128 devices: a whole 4x4x4 slice. The times are simulated.
128 devices in a mesh: pix: 16 (over x, y_hi, core), tm: 8 (over y_lo, z).
Axes of the slice: x: 4, y: 4 (y_hi: 2, y_lo: 2; y = y_hi * 2 + y_lo), z: 4, core: 2. Of those that a mesh axis runs over, the one named last changes fastest.
Arguments:
- movie: bfloat16 [32768, 8192], P('pix', 'tm'), may hold values from -6 to 6
- offsets: int32 [8], replicated, may hold values from -129 to 129, as said below
- spatial: bfloat16 [512, 32768], P('tm', 'pix'), may hold values from -6 to 6
- temporal: bfloat16 [512, 8192], P('pix', 'tm'), may hold values from -6 to 6
- step_spatial: float32 [512], replicated, may hold values from 0.3 to 1
- step_temporal: float32 [512], replicated, may hold values from 0.3 to 1
- thresh_spatial: float32 [512], replicated, may hold values from 0.01 to 0.2
- thresh_temporal: float32 [512], replicated, may hold values from 0.01 to 0.2
Outputs:
- spatial_out: bfloat16 [512, 32768], P('tm', 'pix')
- temporal_out: bfloat16 [512, 8192], P('pix', 'tm')
Inputs may be any that keep to these rules, and one draw needn't show every extreme that they name: `offsets`: every offset is a nonzero pixel step of magnitude at most 129; both 129 and -129 occur among them.
All inputs are finite; a program needn't handle non-finite values.
Results may differ from a plain program's by a relative error of at most 0.0052.
Values may be sent and summed in bfloat16 or wider, within the bound.
No kernel may reach another device: no remote copies, remote signals or barrier semaphores. Data moves between devices by JAX's collectives and lax.ppermute only.
A program may use at most 64 MiB of HBM per device.

v0:
```python
import math

import jax
import jax.numpy as jnp
from jax import lax
from jax.sharding import PartitionSpec as P

HALO = 129
NBR = 8
ROUNDS = 2


def padded_2(array, sides, width):
    for axis, dim in sides:
        size, length = (lax.axis_size(axis), array.shape[dim])
        up = [(i, (i + 1) % size) for i in range(size - 1)]
        down = [(j, i) for i, j in up]
        last = lax.slice_in_dim(array, length - width, length, axis=dim)
        initial = lax.slice_in_dim(array, 0, width, axis=dim)
        before = lax.ppermute(last, axis, up)
        after = lax.ppermute(initial, axis, down)
        array = jnp.concatenate([before, array, after], axis=dim)
    return array


def soften(values, limit):
    return values - jnp.clip(values, -limit, limit)


def contrast(movie, offsets):
    count = movie.shape[0]
    padded = padded_2(movie, (("pix", 0),), HALO)
    total = jnp.zeros(movie.shape, jnp.float32)
    for neighbour in range(NBR):
        begin = HALO + offsets[neighbour]
        shifted = lax.dynamic_slice_in_dim(padded, begin, count, 0)
        total = total + shifted.astype(jnp.float32)
    return (movie.astype(jnp.float32) - total / NBR).astype(jnp.bfloat16)


def residual(contrasted, spatial_full, temporal_full, rank):
    model = lax.dot_general(
        spatial_full, temporal_full, (((0,), (0,)), ((), ())), preferred_element_type=jnp.float32
    )
    return (contrasted.astype(jnp.float32) - model * (1.0 / math.sqrt(rank))).astype(jnp.bfloat16)


def per_device(
    movie, offsets, spatial, temporal, step_spatial, step_temporal, thresh_spatial, thresh_temporal
):
    spatial_rows = spatial.shape[0]
    temporal_rows = temporal.shape[0]
    rank = spatial_rows * lax.axis_size("tm")
    pixels = movie.shape[0] * lax.axis_size("pix")
    frames = movie.shape[1] * lax.axis_size("tm")
    contrasted = contrast(movie, offsets)
    spatial_full = lax.all_gather(spatial, "tm", axis=0, tiled=True)
    temporal_full = lax.all_gather(temporal, "pix", axis=0, tiled=True)
    coef_temporal = step_temporal * (math.sqrt(rank) / pixels)
    coef_spatial = step_spatial * (math.sqrt(rank) / frames)
    temporal_first = lax.axis_index("pix") * temporal_rows
    spatial_first = lax.axis_index("tm") * spatial_rows
    for turn in range(ROUNDS):
        errors = residual(contrasted, spatial_full, temporal_full, rank)
        grad_temporal = lax.psum(
            jnp.dot(spatial_full, errors, preferred_element_type=jnp.float32), "pix"
        )
        temporal_full = soften(
            temporal_full.astype(jnp.float32) + coef_temporal[:, None] * grad_temporal,
            thresh_temporal[:, None],
        ).astype(jnp.bfloat16)
        errors = residual(contrasted, spatial_full, temporal_full, rank)
        partial_spatial = lax.dot_general(
            temporal_full, errors, (((1,), (1,)), ((), ())), preferred_element_type=jnp.float32
        )
        grad_spatial = lax.psum(partial_spatial, "tm")
        spatial_full = soften(
            spatial_full.astype(jnp.float32) + coef_spatial[:, None] * grad_spatial,
            thresh_spatial[:, None],
        ).astype(jnp.bfloat16)
    spatial_out = lax.dynamic_slice_in_dim(spatial_full, spatial_first, spatial_rows, 0)
    temporal_out = lax.dynamic_slice_in_dim(temporal_full, temporal_first, temporal_rows, 0)
    return (spatial_out, temporal_out)


def solution(mesh):
    placed = (P("pix", "tm"), P(), P("tm", "pix"), P("pix", "tm"), P(), P(), P(), P())
    return jax.shard_map(
        per_device,
        mesh=mesh,
        in_specs=placed,
        out_specs=(P("tm", "pix"), P("pix", "tm")),
        check_vma=False,
    )
```

profile of v0, /device:TPU:0, one launch (start us, length us, event | category | flops | bytes accessed | tf_op | source)
XLA Modules:
  0.0 656.1 jit_solution(3651057395726386924)
XLA Ops:
  7.2 0.7 all-gather.5.cloned.1.call-update
  7.9 0.7 all-gather.3.cloned.1.call-update
  8.7 1.1 fusion.12
  9.8 1.3 collective-permute-start
  11.1 1.3 collective-permute-start.1
  12.4 1.6 fusion.13
  24.1 24.4 %concatenate.3 = bf16[2306,1024]{1,0:T(8,128)(2,1)} concatenate(bf16[129,1024]{1,0:T(8,128)(2,1)S(1)} %collective-permute-done, bf16[2048,1024]{1,0:T(8,128)(2,1)} %param.8, bf16[129,1024]{1,0:T(8,128)(2,1)S(1)} %collective-permute-done.1), dimensions={0} | concatenate | bytes 9445376 | tf_op jit(solution)/shard_map/concatenate | solution.py:22
  48.5 19.5 %subtract_convert_fusion = bf16[2048,1024]{1,0:T(8,128)(2,1)} fusion(bf16[2048,1024]{1,0:T(8,128)(2,1)} %param.8, bf16[2306,1024]{1,0:T(8,128)(2,1)} %concatenate.3, s32[]{:T(128)S(6)} %select_n.37, s32[]{:T(128)S(6)} %select_n.36, s32[]{:T(128)S(6)} %select_n.35, s32[]{:T(128)S(6)} %select_n.34, s32[]{:T(128)S(6)} %select_n.33, s32[]{:T(128)S(6)} %select_n.32, ...), kind=kLoop, calls=%fused_computation.8 | loop fusion | flops 39845888 | bytes 41943072 | tf_op jit(solution)/shard_map/convert_element_type | solution.py:38
  68.1 32.1 %all-gather.3.cloned.1.call-done = bf16[512,2048]{1,0:T(8,128)(2,1)} async-done(((bf16[64,2048]{1,0:T(8,128)(2,1)}), bf16[512,2048]{1,0:T(8,128)(2,1)}) %all-gather.3.cloned.1.call-update) | async-done | bytes 2097168 | tf_op jit(solution)/shard_map/all_gather | solution.py:57
  100.2 9.9 %convolution_bitcast_fusion = f32[512,1024]{0,1:T(8,128)} fusion(bf16[512,2048]{1,0:T(8,128)(2,1)} %all-gather.3.cloned.1.call-done, bf16[2048,1024]{1,0:T(8,128)(2,1)} %subtract_convert_fusion, bf16[512,1024]{1,0:T(8,128)(2,1)} %all-gather.5.cloned.1.call-done), kind=kOutput, calls=%fused_computation.12 | convolution fusion | flops 4303355904 | bytes 9437184 | tf_op jit(solution)/shard_map/dot_general | solution.py:66
  111.0 143.3 %all-reduce.5.cloned.1.call-done = f32[512,1024]{0,1:T(8,128)} async-done(((f32[512,1024]{0,1:T(8,128)}), f32[512,1024]{0,1:T(8,128)}) %all-reduce.5.cloned.1.call-update) | async-done | bytes 2097168 | tf_op jit(solution)/shard_map/psum | solution.py:65
  254.2 2.1 subtract_convert_fusion.3
  256.3 9.8 %fusion.6 = f32[512,2048]{1,0:T(8,128)} fusion(bf16[512,1024]{0,1:T(8,128)(2,1)S(1)} %subtract_convert_fusion.3, bf16[2048,1024]{1,0:T(8,128)(2,1)} %subtract_convert_fusion, bf16[512,2048]{1,0:T(8,128)(2,1)} %all-gather.3.cloned.1.call-done), kind=kOutput, calls=%fused_computation.15 | convolution fusion | flops 4303355904 | bytes 11534336 | tf_op jit(solution)/shard_map/dot_general | solution.py:73
  266.2 0.6 copy-done.2
  266.8 105.4 %all-reduce.7.cloned.1.call-done = f32[512,2048]{1,0:T(8,128)} async-done(((f32[512,2048]{1,0:T(8,128)}), f32[512,2048]{1,0:T(8,128)}) %all-reduce.7.cloned.1.call-update) | async-done | bytes 4194320 | tf_op jit(solution)/shard_map/psum | solution.py:76
  372.2 3.9 subtract_convert_fusion.1
  376.1 8.5 %fusion.5 = f32[512,1024]{0,1:T(8,128)} fusion(bf16[512,2048]{1,0:T(8,128)(2,1)S(1)} %subtract_convert_fusion.1, bf16[2048,1024]{1,0:T(8,128)(2,1)} %subtract_convert_fusion, bf16[512,1024]{0,1:T(8,128)(2,1)S(1)} %subtract_convert_fusion.3), kind=kOutput, calls=%fused_computation.14 | convolution fusion | flops 4303355904 | bytes 9437184 | tf_op jit(solution)/shard_map/dot_general | solution.py:66
  384.9 143.6 %all-reduce.9.cloned.1.call-done = f32[512,1024]{0,1:T(8,128)} async-done(((f32[512,1024]{0,1:T(8,128)}), f32[512,1024]{0,1:T(8,128)}) %all-reduce.9.cloned.1.call-update) | async-done | bytes 2097168 | tf_op jit(solution)/shard_map/psum | solution.py:65
  528.5 3.0 subtract_convert_fusion.2
  531.5 9.7 %fusion.4 = f32[512,2048]{1,0:T(8,128)} fusion(bf16[512,1024]{0,1:T(8,128)(2,1)} %subtract_convert_fusion.2, bf16[2048,1024]{1,0:T(8,128)(2,1)} %subtract_convert_fusion, bf16[512,2048]{1,0:T(8,128)(2,1)S(1)} %subtract_convert_fusion.1), kind=kOutput, calls=%fused_computation.13 | convolution fusion | flops 4303355904 | bytes 11534336 | tf_op jit(solution)/shard_map/dot_general | solution.py:73
  541.5 1.1 constant_dynamic-slice_fusion
  542.6 0.8 copy.15
  543.3 104.0 %all-reduce.11.cloned.1.call-done = f32[512,2048]{1,0:T(8,128)} async-done(((f32[512,2048]{1,0:T(8,128)}), f32[512,2048]{1,0:T(8,128)}) %all-reduce.11.cloned.1.call-update) | async-done | bytes 4194320 | tf_op jit(solution)/shard_map/psum | solution.py:76
  647.3 1.9 subtract_convert_fusion.4
  (30 shorter events, 1.5 us)
Async XLA Ops:
  7.2 60.9 %all-gather.5.cloned.1.call-start = ((), (), s32[]{:S(2)}) async-start(), calls=%async_computation.1 | async-start | bytes 1114112 | tf_op jit(solution)/shard_map/all_gather | solution.py:58
  7.9 92.3 %all-gather.3.cloned.1.call-start = ((), (), s32[]{:S(2)}) async-start(), calls=%async_computation | async-start | bytes 2359296 | tf_op jit(solution)/shard_map/all_gather | solution.py:57
  8.6 245.6 %all-reduce.5.cloned.1.call-start = ((), (), s32[]{:S(2)}) async-start(), calls=%async_computation.2 | async-start | bytes 4194304 | tf_op jit(solution)/shard_map/psum | solution.py:65
  9.8 14.2 %collective-permute-start = (bf16[129,1024]{1,0:T(8,128)(2,1)S(1)}, bf16[129,1024]{1,0:T(8,128)(2,1)S(1)}, u32[]{:S(2)}, u32[]{:S(2)}) collective-permute-start(bf16[129,1024]{1,0:T(8,128)(2,1)S(1)} %get-tuple-element.7), channel_id=1, source_target_pairs={{0,8},{8,16},{16,24},{24,32},{32,40},{40,48},{48,56},{56,64},{64,7... | collective-permute-start | bytes 792584 | tf_op jit(solution)/shard_map/ppermute | solution.py:20
  11.1 12.9 %collective-permute-start.1 = (bf16[129,1024]{1,0:T(8,128)(2,1)S(1)}, bf16[129,1024]{1,0:T(8,128)(2,1)S(1)}, u32[]{:S(2)}, u32[]{:S(2)}) collective-permute-start(bf16[129,1024]{1,0:T(8,128)(2,1)S(1)} %get-tuple-element.6), channel_id=1, source_target_pairs={{8,0},{16,8},{24,16},{32,24},{40,32},{48,40},{56,48},{64,56},{72,6... | collective-permute-start | bytes 792584 | tf_op jit(solution)/shard_map/ppermute | solution.py:21
  68.0 42.3 %copy-start.1 = (f32[512]{0:T(512)S(1)}, f32[512]{0:T(512)}, u32[]{:S(2)}) copy-start(f32[512]{0:T(512)} %param.15) | copy-start | bytes 6148
  68.0 42.4 %copy-start.3 = (f32[512]{0:T(512)S(1)}, f32[512]{0:T(512)}, u32[]{:S(2)}) copy-start(f32[512]{0:T(512)} %param.13) | copy-start | bytes 6148
  68.1 42.4 %copy-start = (bf16[512,1024]{1,0:T(8,128)(2,1)S(1)}, bf16[512,1024]{1,0:T(8,128)(2,1)}, u32[]{:S(2)}) copy-start(bf16[512,1024]{1,0:T(8,128)(2,1)} %all-gather.5.cloned.1.call-done) | copy-start | bytes 3145732
  110.1 262.1 %all-reduce.7.cloned.1.call-start = ((), (), s32[]{:S(2)}) async-start(), calls=%async_computation.3 | async-start | bytes 8388608 | tf_op jit(solution)/shard_map/psum | solution.py:76
  266.1 0.7 copy-start.2
  266.1 0.7 copy-start.4
  266.1 262.3 %all-reduce.9.cloned.1.call-start = ((), (), s32[]{:S(2)}) async-start(), calls=%async_computation.4 | async-start | bytes 4194304 | tf_op jit(solution)/shard_map/psum | solution.py:65
  384.6 262.7 %all-reduce.11.cloned.1.call-start = ((), (), s32[]{:S(2)}) async-start(), calls=%async_computation.5 | async-start | bytes 8388608 | tf_op jit(solution)/shard_map/psum | solution.py:76
Sparse Core Ops, SparseCore 0:
  10.4 47.3 all-gather.4
  59.5 40.6 all-gather.2
  110.3 143.9 all-reduce.4
  266.3 105.9 all-reduce.6
  384.7 143.7 all-reduce.8
  541.4 105.9 all-reduce.10
where the time goes:
time: 658 us; the launch traced here: 656 us
  waiting for transfers between devices  530 us (81%)
  matrix products  37.9 us (6%)
  local copies, waits for them, and re-layouts  30.4 us (5%)
  other arithmetic  30.4 us (5%)
  between operations  24.2 us (4%)
    psum x2, waiting for transfers between devices, per_device(): lax.psum(jnp.dot(spatial_full, errors, preferred_element_type=jnp.float32...  287 us
    psum x2, waiting for transfers between devices, per_device(): grad_spatial = lax.psum(partial_spatial, 'tm')  209 us
    all_gather x1, waiting for transfers between devices, per_device(): spatial_full = lax.all_gather(spatial, 'tm', axis=0, tiled=True)  32.1 us
    concatenate x1, local copies, waits for them, and re-layouts, padded_2(): array = jnp.concatenate([before, array, after], axis=dim)  24.4 us
    dot_general x2, matrix products, per_device(): lax.dot_general(temporal_full, errors, (((1,), (1,)), ((), ())), preferre...  19.5 us
    convert_element_type x1, other arithmetic, contrast(): return (movie.astype(jnp.float32) - total / NBR).astype(jnp.bfloat16)  19.5 us
    dot_general x2, matrix products, per_device(): jnp.dot(spatial_full, errors, preferred_element_type=jnp.float32)  18.4 us
  transfers between devices with their start and end apart: 8, of which 5 were waited for; matrix products, arithmetic and copies ran while one was open for 8% of the time, Pallas kernels for 0%

commit v1 on v0

v1 whole, which is shorter than its diff:
```python
import functools
import math

import jax
import jax.numpy as jnp
from jax import lax
from jax.experimental import pallas as pl
from jax.experimental.pallas import tpu as pltpu
from jax.sharding import PartitionSpec as P

HALO = 129
EDGE = 144
BLOCK = 256
NBR = 8
ROUNDS = 2
BF16 = jnp.bfloat16
F32 = jnp.float32


def pix_pairs(move):
    pairs = []
    for x in range(4):
        for y in range(2):
            for c in range(2):
                to = move(x, y, c)
                pairs.append((x * 4 + y * 2 + c, (to[0] % 4) * 4 + (to[1] % 2) * 2 + to[2] % 2))
    return pairs


def tm_pairs(move):
    pairs = []
    for y in range(2):
        for z in range(4):
            to = move(y, z)
            pairs.append((y * 4 + z, (to[0] % 2) * 4 + to[1] % 4))
    return pairs


def by_core(a):
    return lax.ppermute(a, "pix", pix_pairs(lambda x, y, c: (x, y, c + 1)))


def by_yhi(a):
    return lax.ppermute(a, "pix", pix_pairs(lambda x, y, c: (x, y + 1, c)))


def by_x(a, d):
    return lax.ppermute(a, "pix", pix_pairs(lambda x, y, c: (x + d, y, c)))


def by_ylo(a):
    return lax.ppermute(a, "tm", tm_pairs(lambda y, z: (y + 1, z)))


def by_z(a, d):
    return lax.ppermute(a, "tm", tm_pairs(lambda y, z: (y, z + d)))


def pick(a, index, axis):
    return lax.dynamic_index_in_dim(a, index, axis, keepdims=False)


def gather_pair(own, here, send, axis):
    other = send(own)
    low = jnp.where(here == 0, own, other)
    high = jnp.where(here == 0, other, own)
    return jnp.stack([low, high], axis)


def gather_four(own, here, send, axis):
    got = [own] + [send(own, d) for d in (1, 2, 3)]
    slots = []
    for k in range(4):
        slots.append(lax.select_n(jnp.mod(here - k, 4), *got))
    return jnp.stack(slots, axis)


def reduce_pair(a, here, send, axis):
    got = send(pick(a, 1 - here, axis).astype(BF16))
    return pick(a, here, axis) + got.astype(F32)


def reduce_four(a, here, send, axis):
    total = pick(a, here, axis)
    got = [send(pick(a, jnp.mod(here + d, 4), axis).astype(BF16), d) for d in (1, 2, 3)]
    for g in got:
        total = total + g.astype(F32)
    return total


def soften(values, limit):
    return values - jnp.clip(values, -limit, limit)


def stencil(offsets_ref, movie_ref, before_ref, after_ref, out_ref):
    def band(columns, base):
        step = (
            lax.broadcasted_iota(jnp.int32, (BLOCK, columns), 1)
            - lax.broadcasted_iota(jnp.int32, (BLOCK, columns), 0)
            + base
        )
        weight = jnp.where(step == 0, 1.0, 0.0).astype(F32)
        for k in range(NBR):
            weight = weight - jnp.where(step == offsets_ref[k], 1.0 / NBR, 0.0).astype(F32)
        return weight.astype(BF16)

    rows = movie_ref.shape[0]
    blocks = rows // BLOCK
    main = band(3 * BLOCK, -BLOCK)
    for b in range(blocks):
        low = max(b - 1, 0) * BLOCK
        high = min(b + 2, blocks) * BLOCK
        first = low - (b - 1) * BLOCK
        total = jnp.dot(
            main[:, first : first + high - low], movie_ref[low:high, :], preferred_element_type=F32
        )
        if b == 0:
            total += jnp.dot(band(EDGE, -EDGE), before_ref[...], preferred_element_type=F32)
        if b == blocks - 1:
            total += jnp.dot(band(EDGE, BLOCK), after_ref[...], preferred_element_type=F32)
        out_ref[b * BLOCK : (b + 1) * BLOCK, :] = total.astype(BF16)


def contrast(movie, offsets):
    size = lax.axis_size("pix")
    rows = movie.shape[0]
    up = [(i, i + 1) for i in range(size - 1)]
    down = [(j, i) for i, j in up]
    before = lax.ppermute(movie[rows - EDGE :], "pix", up)
    after = lax.ppermute(movie[:EDGE], "pix", down)
    vmem = pl.BlockSpec(memory_space=pltpu.VMEM)
    return pl.pallas_call(
        stencil,
        out_shape=jax.ShapeDtypeStruct(movie.shape, BF16),
        in_specs=[pl.BlockSpec(memory_space=pltpu.SMEM), vmem, vmem, vmem],
        out_specs=vmem,
        compiler_params=pltpu.CompilerParams(vmem_limit_bytes=32 * 1024 * 1024),
    )(offsets, movie, before, after)


def dot(a, b, over):
    return lax.dot_general(a, b, ((over[0], over[1]), ((), ())), preferred_element_type=F32)


def per_device(
    movie, offsets, spatial, temporal, step_spatial, step_temporal, thresh_spatial, thresh_temporal
):
    spatial_rows, strip = spatial.shape
    temporal_rows, span = temporal.shape
    rank = spatial_rows * lax.axis_size("tm")
    pixels = strip * lax.axis_size("pix")
    frames = span * lax.axis_size("tm")
    half = strip // 2
    pix = lax.axis_index("pix")
    tm = lax.axis_index("tm")
    x, yhi, core = pix // 4, (pix // 2) % 2, pix % 2
    ylo, z = tm // 4, tm % 4

    def own(a, index, rows):
        return lax.dynamic_slice_in_dim(a, index * rows, rows, 0)[:, None]

    coef_temporal = own(step_temporal * (math.sqrt(rank) / pixels), pix, temporal_rows)
    coef_spatial = own(step_spatial * (math.sqrt(rank) / frames), tm, spatial_rows)
    limit_temporal = own(thresh_temporal, pix, temporal_rows)
    limit_spatial = own(thresh_spatial, tm, spatial_rows)
    scale = 1.0 / math.sqrt(rank)

    def gather_temporal(t):
        a = gather_pair(t, yhi, by_yhi, 0)
        a = gather_four(a, x, by_x, 0)
        a = gather_pair(a, core, by_core, 2)
        return a.reshape(rank, span)

    def gather_spatial(sa, sb):
        a = gather_pair(sa, ylo, by_ylo, 0)
        b = gather_four(sb, z, by_z, 0)
        a = gather_four(a, z, by_z, 1)
        b = gather_pair(b, ylo, by_ylo, 0)
        return a.reshape(rank, half), b.reshape(rank, half)

    def reduce_temporal(g):
        g = g.reshape(4, 2, 2, temporal_rows, span)
        g = reduce_pair(g, core, by_core, 2)
        g = reduce_four(g, x, by_x, 0)
        return reduce_pair(g, yhi, by_yhi, 0)

    def reduce_spatial(ga, gb):
        ga = ga.reshape(2, 4, spatial_rows, half)
        gb = gb.reshape(2, 4, spatial_rows, half)
        ga = reduce_four(ga, z, by_z, 1)
        gb = reduce_pair(gb, ylo, by_ylo, 0)
        ga = reduce_pair(ga, ylo, by_ylo, 0)
        gb = reduce_four(gb, z, by_z, 0)
        return ga, gb

    sa, sb = spatial[:, :half], spatial[:, half:]
    t = temporal
    full_a, full_b = gather_spatial(sa, sb)
    full_t = gather_temporal(t)
    contrasted = contrast(movie, offsets)
    ca, cb = contrasted[:half], contrasted[half:]
    for turn in range(ROUNDS):
        gram = dot(full_a, full_a, ((1,), (1,))) + dot(full_b, full_b, ((1,), (1,)))
        cross = dot(full_a, ca, ((1,), (0,))) + dot(full_b, cb, ((1,), (0,)))
        grad = cross - dot((gram * scale).astype(BF16), full_t, ((1,), (0,)))
        grad = reduce_temporal(grad)
        t = soften(t.astype(F32) + coef_temporal * grad, limit_temporal).astype(BF16)
        full_t = gather_temporal(t)
        gram = (dot(full_t, full_t, ((1,), (1,))) * scale).astype(BF16)
        grad_a = dot(full_t, ca, ((1,), (1,))) - dot(gram, full_a, ((1,), (0,)))
        grad_b = dot(full_t, cb, ((1,), (1,))) - dot(gram, full_b, ((1,), (0,)))
        grad_a, grad_b = reduce_spatial(grad_a, grad_b)
        sa = soften(sa.astype(F32) + coef_spatial * grad_a, limit_spatial).astype(BF16)
        sb = soften(sb.astype(F32) + coef_spatial * grad_b, limit_spatial).astype(BF16)
        if turn < ROUNDS - 1:
            full_a, full_b = gather_spatial(sa, sb)
    return jnp.concatenate([sa, sb], 1), t


def solution(mesh):
    placed = (P("pix", "tm"), P(), P("tm", "pix"), P("pix", "tm"), P(), P(), P(), P())
    return jax.shard_map(
        per_device,
        mesh=mesh,
        in_specs=placed,
        out_specs=(P("tm", "pix"), P("pix", "tm")),
        check_vma=False,
    )
```

time: 658 us -> 254 us (0.39)
  waiting for transfers between devices: 530 us -> 118 us
  starting transfers between devices: 3.24 us -> 73.9 us
  local copies, waits for them, and re-layouts: 30.4 us -> 6.4 us
  between operations: 24.2 us -> 1.99 us
  other arithmetic: 30.4 us -> 9.37 us
    psum x4 -> x0, waiting for transfers between devices: 496 us -> none  [the longest x2 287 us: per_device(): lax.psum(jnp.dot(spatial_full, errors, preferred_element_type=jnp.float32...]
    ppermute x2 -> x59, waiting for transfers between devices: 0.01 us -> 118 us  [the longest x24 50.9 us: by_z(): return lax.ppermute(a, 'tm', tm_pairs(lambda y, z: (y, z + d)))]
    ppermute x2 -> x59, starting transfers between devices: 2.6 us -> 73.9 us  [the longest x24 37.2 us: by_z(): return lax.ppermute(a, 'tm', tm_pairs(lambda y, z: (y, z + d)))]
    all_gather x2 -> x0, waiting for transfers between devices: 32.2 us -> none  [the longest x1 32.1 us: per_device(): spatial_full = lax.all_gather(spatial, 'tm', axis=0, tiled=True)]
    convert_element_type x5 -> x4, other arithmetic: 30.4 us -> 0.68 us  [the longest x1 0.24 us: per_device(): soften(sb.astype(F32) + coef_spatial * grad_b, limit_spatial).astype(BF16)]
    concatenate x1 -> x0, local copies, waits for them, and re-layouts: 24.4 us -> none  [padded_2(): array = jnp.concatenate([before, array, after], axis=dim)]
    dot_general x4 -> x18, matrix products: 37.9 us -> 34.5 us  [dot(): lax.dot_general(a, b, ((over[0], over[1]), ((), ())), preferred_element_t...]
  transfers between devices with their start and end apart: 8 -> 59, of which waited for: 5 -> 43; matrix products, arithmetic and copies ran while one was open for 8% -> 5% of each run, Pallas kernels for 0% -> 2%
where the time goes in v1:
time: 254 us; the launch traced here: 249 us
  waiting for transfers between devices  118 us (46%)
  starting transfers between devices  73.9 us (29%)
  matrix products  34.5 us (14%)
  other arithmetic  9.37 us (4%)
  local copies, waits for them, and re-layouts  6.4 us (3%)
  Pallas kernels  4.83 us (2%)
    ppermute x24, waiting for transfers between devices, by_z(): return lax.ppermute(a, 'tm', tm_pairs(lambda y, z: (y, z + d)))  50.9 us
    ppermute x24, starting transfers between devices, by_z(): return lax.ppermute(a, 'tm', tm_pairs(lambda y, z: (y, z + d)))  37.2 us
    dot_general x18, matrix products, dot(): lax.dot_general(a, b, ((over[0], over[1]), ((), ())), preferred_element_t...  34.5 us
    ppermute x15, waiting for transfers between devices, by_x(): return lax.ppermute(a, 'pix', pix_pairs(lambda x, y, c: (x + d, y, c)))  29.1 us
    ppermute x15, starting transfers between devices, by_x(): return lax.ppermute(a, 'pix', pix_pairs(lambda x, y, c: (x + d, y, c)))  22.1 us
    ppermute x5, waiting for transfers between devices, by_yhi(): return lax.ppermute(a, 'pix', pix_pairs(lambda x, y, c: (x, y + 1, c)))  21 us
    ppermute x8, waiting for transfers between devices, by_ylo(): return lax.ppermute(a, 'tm', tm_pairs(lambda y, z: (y + 1, z)))  9.51 us
    ppermute x5, waiting for transfers between devices, by_core(): return lax.ppermute(a, 'pix', pix_pairs(lambda x, y, c: (x, y, c + 1)))  7.88 us
  transfers between devices with their start and end apart: 59, of which 43 were waited for; matrix products, arithmetic and copies ran while one was open for 5% of the time, Pallas kernels for 2%

profile of v1, /device:TPU:0, one launch (start us, length us, event | category | flops | bytes accessed | tf_op | source)
XLA Modules:
  0.0 249.4 jit_solution(18325379463281280175)
XLA Ops:
  10.5 8.5 %collective-permute-start.12 = (bf16[2,32,1024]{2,1,0:T(8,128)(2,1)S(1)}, bf16[2,32,1024]{2,1,0:T(8,128)(2,1)S(1)}, u32[]{:S(2)}, u32[]{:S(2)}) collective-permute-start(bf16[2,32,1024]{2,1,0:T(8,128)(2,1)S(1)} %pad_maximum_fusion.15), channel_id=1, source_target_pairs={{0,64},{8,72},{16,80},{24,88},{32,96},{40,104},{48,112},{56,120},{... | collective-permute-start | bytes 393224 | tf_op jit(solution)/shard_map/ppermute | solution.py:48
  22.7 3.9 %collective-permute-start.7 = (bf16[64,1024]{1,0:T(8,128)(2,1)S(1)}, bf16[64,1024]{1,0:T(8,128)(2,1)S(1)}, u32[]{:S(2)}, u32[]{:S(2)}) collective-permute-start(bf16[64,1024]{1,0:T(8,128)(2,1)S(1)} %get-tuple-element.65), channel_id=1, source_target_pairs={{0,2},{1,3},{2,0},{3,1},{4,6},{5,7},{6,4},{7,5},{8,10},{9,11},{10,... | collective-permute-start | bytes 393224 | tf_op jit(solution)/shard_map/ppermute | solution.py:56
  26.6 4.0 %collective-permute-start.8 = (bf16[64,1024]{1,0:T(8,128)(2,1)S(1)}, bf16[64,1024]{1,0:T(8,128)(2,1)S(1)}, u32[]{:S(2)}, u32[]{:S(2)}) collective-permute-start(bf16[64,1024]{1,0:T(8,128)(2,1)S(1)} %get-tuple-element.65), channel_id=1, source_target_pairs={{0,3},{1,0},{2,1},{3,2},{4,7},{5,4},{6,5},{7,6},{8,11},{9,8},{10,9... | collective-permute-start | bytes 393224 | tf_op jit(solution)/shard_map/ppermute | solution.py:56
  30.8 3.7 %collective-permute-start.2 = (bf16[2,64,1024]{2,1,0:T(8,128)(2,1)S(1)}, bf16[2,64,1024]{2,1,0:T(8,128)(2,1)S(1)}, u32[]{:S(2)}, u32[]{:S(2)}) collective-permute-start(bf16[2,64,1024]{2,1,0:T(8,128)(2,1)S(1)} %pad_maximum_fusion.12), channel_id=1, source_target_pairs={{0,2},{1,3},{2,0},{3,1},{4,6},{5,7},{6,4},{7,5},{8,10},{9,11},{10,... | collective-permute-start | bytes 786440 | tf_op jit(solution)/shard_map/ppermute | solution.py:56
  36.6 4.2 %collective-permute-start.3 = (bf16[2,64,1024]{2,1,0:T(8,128)(2,1)S(1)}, bf16[2,64,1024]{2,1,0:T(8,128)(2,1)S(1)}, u32[]{:S(2)}, u32[]{:S(2)}) collective-permute-start(bf16[2,64,1024]{2,1,0:T(8,128)(2,1)S(1)} %pad_maximum_fusion.12), channel_id=1, source_target_pairs={{0,3},{1,0},{2,1},{3,2},{4,7},{5,4},{6,5},{7,6},{8,11},{9,8},{10,9... | collective-permute-start | bytes 786440 | tf_op jit(solution)/shard_map/ppermute | solution.py:56
  41.4 4.8 %shard_map.95 = bf16[2048,1024]{1,0:T(8,128)(2,1)S(1)} custom-call(s32[8]{0:T(128)S(1)} %copy-done.5, bf16[2048,1024]{1,0:T(8,128)(2,1)S(1)} %copy-done.4, bf16[144,1024]{1,0:T(8,128)(2,1)S(1)} %collective-permute-done.4.before_ref, bf16[144,1024]{1,0:T(8,128)(2,1)S(1)} %collective-permute-done.5.after_ref), custom_call_target="tpu_custom_call" | custom-call | tf_op jit(solution)/shard_map/pallas_call | solution.py:132
  50.6 4.9 %collective-permute-done.9 = bf16[4,64,1024]{2,1,0:T(8,128)(2,1)S(1)} collective-permute-done((bf16[4,64,1024]{2,1,0:T(8,128)(2,1)S(1)}, bf16[4,64,1024]{2,1,0:T(8,128)(2,1)S(1)}, u32[]{:S(2)}, u32[]{:S(2)}) %collective-permute-start.9) | collective-permute-done | bytes 524320 | tf_op jit(solution)/shard_map/ppermute | solution.py:52
  58.4 3.8 %fusion.17 = f32[512,1024]{1,0:T(8,128)} fusion(bf16[512,1024]{1,0:T(8,128)(2,1)S(1)} %bitcast.346, f32[512,512]{1,0:T(8,128)} %fusion.75, bf16[512,1024]{1,0:T(8,128)(2,1)S(1)} %bitcast.330), kind=kOutput, calls=%fused_computation.27 | convolution fusion | flops 1074528256 | bytes 5242880 | tf_op jit(solution)/shard_map/dot_general | solution.py:142
  62.3 4.1 %add_subtract_fusion.1 = f32[512,1024]{1,0:T(8,128)S(1)} fusion(f32[512,1024]{1,0:T(8,128)} %fusion.17, f32[512,1024]{1,0:T(8,128)} %fusion.6, bf16[512,1024]{1,0:T(8,128)(2,1)S(1)} %bitcast.320, bf16[2048,1024]{1,0:T(8,128)(2,1)} %copy-done), kind=kOutput, calls=%fused_computation.1 | convolution fusion | flops 1074790400 | bytes 9437184 | tf_op jit(solution)/shard_map/dot_general | solution.py:142
  74.9 4.8 %collective-permute-done.18 = bf16[2,32,1024]{2,1,0:T(8,128)(2,1)S(1)} collective-permute-done((bf16[2,32,1024]{2,1,0:T(8,128)(2,1)S(1)}, bf16[2,32,1024]{2,1,0:T(8,128)(2,1)S(1)}, u32[]{:S(2)}, u32[]{:S(2)}) %collective-permute-start.18) | collective-permute-done | bytes 131104 | tf_op jit(solution)/shard_map/ppermute | solution.py:48
  84.2 5.0 %collective-permute-done.19 = bf16[32,1024]{1,0:T(8,128)(2,1)S(1)} collective-permute-done((bf16[32,1024]{1,0:T(8,128)(2,1)S(1)}, bf16[32,1024]{1,0:T(8,128)(2,1)S(1)}, u32[]{:S(2)}, u32[]{:S(2)}) %collective-permute-start.19) | collective-permute-done | bytes 65568 | tf_op jit(solution)/shard_map/ppermute | solution.py:44
  89.4 5.8 %collective-permute-done.20 = bf16[32,1024]{1,0:T(8,128)(2,1)S(1)} collective-permute-done((bf16[32,1024]{1,0:T(8,128)(2,1)S(1)}, bf16[32,1024]{1,0:T(8,128)(2,1)S(1)}, u32[]{:S(2)}, u32[]{:S(2)}) %collective-permute-start.20) | collective-permute-done | bytes 65568 | tf_op jit(solution)/shard_map/ppermute | solution.py:44
  97.8 3.9 %collective-permute-done.22 = bf16[2,32,1024]{2,1,0:T(8,128)(2,1)S(1)} collective-permute-done((bf16[2,32,1024]{2,1,0:T(8,128)(2,1)S(1)}, bf16[2,32,1024]{2,1,0:T(8,128)(2,1)S(1)}, u32[]{:S(2)}, u32[]{:S(2)}) %collective-permute-start.22) | collective-permute-done | bytes 131104 | tf_op jit(solution)/shard_map/ppermute | solution.py:48
  117.1 10.1 %collective-permute-done.27 = bf16[2,64,1024]{2,1,0:T(8,128)(2,1)S(1)} collective-permute-done((bf16[2,64,1024]{2,1,0:T(8,128)(2,1)S(1)}, bf16[2,64,1024]{2,1,0:T(8,128)(2,1)S(1)}, u32[]{:S(2)}, u32[]{:S(2)}) %collective-permute-start.27) | collective-permute-done | bytes 262176 | tf_op jit(solution)/shard_map/ppermute | solution.py:56
  127.2 3.4 %collective-permute-done.25 = bf16[2,64,1024]{2,1,0:T(8,128)(2,1)S(1)} collective-permute-done((bf16[2,64,1024]{2,1,0:T(8,128)(2,1)S(1)}, bf16[2,64,1024]{2,1,0:T(8,128)(2,1)S(1)}, u32[]{:S(2)}, u32[]{:S(2)}) %collective-permute-start.25) | collective-permute-done | bytes 262176 | tf_op jit(solution)/shard_map/ppermute | solution.py:56
  170.1 4.1 %fusion.16 = f32[512,1024]{1,0:T(8,128)} fusion(bf16[512,1024]{1,0:T(8,128)(2,1)} %bitcast.342, f32[512,512]{1,0:T(8,128)} %fusion.78, bf16[512,1024]{1,0:T(8,128)(2,1)S(1)} %bitcast.333), kind=kOutput, calls=%fused_computation.26 | convolution fusion | flops 1074528256 | bytes 5242880 | tf_op jit(solution)/shard_map/dot_general | solution.py:142
  174.2 4.1 %add_subtract_fusion = f32[512,1024]{1,0:T(8,128)S(1)} fusion(f32[512,1024]{1,0:T(8,128)} %fusion.16, f32[512,1024]{1,0:T(8,128)} %fusion.3, bf16[512,1024]{1,0:T(8,128)(2,1)S(1)} %bitcast.323, bf16[2048,1024]{1,0:T(8,128)(2,1)} %copy-done), kind=kOutput, calls=%fused_computation | convolution fusion | flops 1074790400 | bytes 9437184 | tf_op jit(solution)/shard_map/dot_general | solution.py:142
  182.9 4.1 %collective-permute-done.44 = bf16[2,32,1024]{2,1,0:T(8,128)(2,1)S(1)} collective-permute-done((bf16[2,32,1024]{2,1,0:T(8,128)(2,1)S(1)}, bf16[2,32,1024]{2,1,0:T(8,128)(2,1)S(1)}, u32[]{:S(2)}, u32[]{:S(2)}) %collective-permute-start.44) | collective-permute-done | bytes 131104 | tf_op jit(solution)/shard_map/ppermute | solution.py:48
  192.2 5.1 %collective-permute-done.45 = bf16[32,1024]{1,0:T(8,128)(2,1)S(1)} collective-permute-done((bf16[32,1024]{1,0:T(8,128)(2,1)S(1)}, bf16[32,1024]{1,0:T(8,128)(2,1)S(1)}, u32[]{:S(2)}, u32[]{:S(2)}) %collective-permute-start.45) | collective-permute-done | bytes 65568 | tf_op jit(solution)/shard_map/ppermute | solution.py:44
  198.2 5.1 %collective-permute-done.46 = bf16[32,1024]{1,0:T(8,128)(2,1)S(1)} collective-permute-done((bf16[32,1024]{1,0:T(8,128)(2,1)S(1)}, bf16[32,1024]{1,0:T(8,128)(2,1)S(1)}, u32[]{:S(2)}, u32[]{:S(2)}) %collective-permute-start.46) | collective-permute-done | bytes 65568 | tf_op jit(solution)/shard_map/ppermute | solution.py:44
  206.0 3.9 %collective-permute-done.48 = bf16[2,32,1024]{2,1,0:T(8,128)(2,1)S(1)} collective-permute-done((bf16[2,32,1024]{2,1,0:T(8,128)(2,1)S(1)}, bf16[2,32,1024]{2,1,0:T(8,128)(2,1)S(1)}, u32[]{:S(2)}, u32[]{:S(2)}) %collective-permute-start.48) | collective-permute-done | bytes 131104 | tf_op jit(solution)/shard_map/ppermute | solution.py:48
  223.9 3.5 %collective-permute-done.53 = bf16[2,64,1024]{2,1,0:T(8,128)(2,1)S(1)} collective-permute-done((bf16[2,64,1024]{2,1,0:T(8,128)(2,1)S(1)}, bf16[2,64,1024]{2,1,0:T(8,128)(2,1)S(1)}, u32[]{:S(2)}, u32[]{:S(2)}) %collective-permute-start.53) | collective-permute-done | bytes 262176 | tf_op jit(solution)/shard_map/ppermute | solution.py:56
  230.1 4.5 %collective-permute-done.51 = bf16[2,64,1024]{2,1,0:T(8,128)(2,1)S(1)} collective-permute-done((bf16[2,64,1024]{2,1,0:T(8,128)(2,1)S(1)}, bf16[2,64,1024]{2,1,0:T(8,128)(2,1)S(1)}, u32[]{:S(2)}, u32[]{:S(2)}) %collective-permute-start.51) | collective-permute-done | bytes 262176 | tf_op jit(solution)/shard_map/ppermute | solution.py:56
  236.7 3.7 %collective-permute-start.58 = (bf16[64,1024]{1,0:T(8,128)(2,1)S(1)}, bf16[64,1024]{1,0:T(8,128)(2,1)S(1)}, u32[]{:S(2)}, u32[]{:S(2)}) collective-permute-start(bf16[64,1024]{1,0:T(8,128)(2,1)S(1)} %get-tuple-element.15), channel_id=1, source_target_pairs={{0,3},{1,0},{2,1},{3,2},{4,7},{5,4},{6,5},{7,6},{8,11},{9,8},{10,9... | collective-permute-start | bytes 393224 | tf_op jit(solution)/shard_map/ppermute | solution.py:56
  (224 shorter events, 134.3 us)
Async XLA Ops:
  4.9 15.2 %collective-permute-start = (bf16[64,1024]{1,0:T(8,128)(2,1)S(1)}, bf16[64,1024]{1,0:T(8,128)(2,1)S(1)}, u32[]{:S(2)}, u32[]{:S(2)}) collective-permute-start(bf16[64,1024]{1,0:T(8,128)(2,1)S(1)} %slice.18), channel_id=1, source_target_pairs={{0,4},{1,5},{2,6},{3,7},{4,0},{5,1},{6,2},{7,3},{8,12},{9,13},{10,... | collective-permute-start | bytes 393224 | tf_op jit(solution)/shard_map/ppermute | solution.py:52
  6.8 34.2 %collective-permute-start.4 = (bf16[144,1024]{1,0:T(8,128)(2,1)S(1)}, bf16[144,1024]{1,0:T(8,128)(2,1)S(1)}, u32[]{:S(2)}, u32[]{:S(2)}) collective-permute-start(bf16[144,1024]{1,0:T(8,128)(2,1)S(1)} %get-tuple-element.7), channel_id=1, source_target_pairs={{0,8},{8,16},{16,24},{24,32},{32,40},{40,48},{48,56},{56,64},{64,7... | collective-permute-start | bytes 884744 | tf_op jit(solution)/shard_map/ppermute | solution.py:129
  8.1 33.0 %collective-permute-start.5 = (bf16[144,1024]{1,0:T(8,128)(2,1)S(1)}, bf16[144,1024]{1,0:T(8,128)(2,1)S(1)}, u32[]{:S(2)}, u32[]{:S(2)}) collective-permute-start(bf16[144,1024]{1,0:T(8,128)(2,1)S(1)} %get-tuple-element.6), channel_id=1, source_target_pairs={{8,0},{16,8},{24,16},{32,24},{40,32},{48,40},{56,48},{64,56},{72,6... | collective-permute-start | bytes 884744 | tf_op jit(solution)/shard_map/ppermute | solution.py:130
  10.5 12.2 %collective-permute-start.12 = (bf16[2,32,1024]{2,1,0:T(8,128)(2,1)S(1)}, bf16[2,32,1024]{2,1,0:T(8,128)(2,1)S(1)}, u32[]{:S(2)}, u32[]{:S(2)}) collective-permute-start(bf16[2,32,1024]{2,1,0:T(8,128)(2,1)S(1)} %pad_maximum_fusion.15), channel_id=1, source_target_pairs={{0,64},{8,72},{16,80},{24,88},{32,96},{40,104},{48,112},{56,120},{... | collective-permute-start | bytes 393224 | tf_op jit(solution)/shard_map/ppermute | solution.py:48
  20.1 10.4 %collective-permute-start.11 = (bf16[2,32,1024]{2,1,0:T(8,128)(2,1)S(1)}, bf16[2,32,1024]{2,1,0:T(8,128)(2,1)S(1)}, u32[]{:S(2)}, u32[]{:S(2)}) collective-permute-start(bf16[2,32,1024]{2,1,0:T(8,128)(2,1)S(1)} %pad_maximum_fusion.15), channel_id=1, source_target_pairs={{0,32},{8,40},{16,48},{24,56},{32,64},{40,72},{48,80},{56,88},{64,... | collective-permute-start | bytes 393224 | tf_op jit(solution)/shard_map/ppermute | solution.py:48
  26.6 10.1 %collective-permute-start.8 = (bf16[64,1024]{1,0:T(8,128)(2,1)S(1)}, bf16[64,1024]{1,0:T(8,128)(2,1)S(1)}, u32[]{:S(2)}, u32[]{:S(2)}) collective-permute-start(bf16[64,1024]{1,0:T(8,128)(2,1)S(1)} %get-tuple-element.65), channel_id=1, source_target_pairs={{0,3},{1,0},{2,1},{3,2},{4,7},{5,4},{6,5},{7,6},{8,11},{9,8},{10,9... | collective-permute-start | bytes 393224 | tf_op jit(solution)/shard_map/ppermute | solution.py:56
  30.6 10.3 %collective-permute-start.6 = (bf16[64,1024]{1,0:T(8,128)(2,1)S(1)}, bf16[64,1024]{1,0:T(8,128)(2,1)S(1)}, u32[]{:S(2)}, u32[]{:S(2)}) collective-permute-start(bf16[64,1024]{1,0:T(8,128)(2,1)S(1)} %get-tuple-element.65), channel_id=1, source_target_pairs={{0,1},{1,2},{2,3},{3,0},{4,5},{5,6},{6,7},{7,4},{8,9},{9,10},{10,1... | collective-permute-start | bytes 393224 | tf_op jit(solution)/shard_map/ppermute | solution.py:56
  30.8 15.5 %collective-permute-start.2 = (bf16[2,64,1024]{2,1,0:T(8,128)(2,1)S(1)}, bf16[2,64,1024]{2,1,0:T(8,128)(2,1)S(1)}, u32[]{:S(2)}, u32[]{:S(2)}) collective-permute-start(bf16[2,64,1024]{2,1,0:T(8,128)(2,1)S(1)} %pad_maximum_fusion.12), channel_id=1, source_target_pairs={{0,2},{1,3},{2,0},{3,1},{4,6},{5,7},{6,4},{7,5},{8,10},{9,11},{10,... | collective-permute-start | bytes 786440 | tf_op jit(solution)/shard_map/ppermute | solution.py:56
  36.6 9.6 %collective-permute-start.3 = (bf16[2,64,1024]{2,1,0:T(8,128)(2,1)S(1)}, bf16[2,64,1024]{2,1,0:T(8,128)(2,1)S(1)}, u32[]{:S(2)}, u32[]{:S(2)}) collective-permute-start(bf16[2,64,1024]{2,1,0:T(8,128)(2,1)S(1)} %pad_maximum_fusion.12), channel_id=1, source_target_pairs={{0,3},{1,0},{2,1},{3,2},{4,7},{5,4},{6,5},{7,6},{8,11},{9,8},{10,9... | collective-permute-start | bytes 786440 | tf_op jit(solution)/shard_map/ppermute | solution.py:56
  41.0 9.4 %collective-permute-start.14 = (bf16[4,2,32,1024]{3,2,1,0:T(8,128)(2,1)S(1)}, bf16[4,2,32,1024]{3,2,1,0:T(8,128)(2,1)S(1)}, u32[]{:S(2)}, u32[]{:S(2)}) collective-permute-start(bf16[4,2,32,1024]{3,2,1,0:T(8,128)(2,1)S(1)} %pad_maximum_fusion.8), channel_id=1, source_target_pairs={{0,8},{8,0},{16,24},{24,16},{32,40},{40,32},{48,56},{56,48},{64,72... | collective-permute-start | bytes 1572872 | tf_op jit(solution)/shard_map/ppermute | solution.py:40
  41.1 14.5 %collective-permute-start.9 = (bf16[4,64,1024]{2,1,0:T(8,128)(2,1)S(1)}, bf16[4,64,1024]{2,1,0:T(8,128)(2,1)S(1)}, u32[]{:S(2)}, u32[]{:S(2)}) collective-permute-start(bf16[4,64,1024]{2,1,0:T(8,128)(2,1)S(1)} %pad_maximum_fusion.7), channel_id=1, source_target_pairs={{0,4},{1,5},{2,6},{3,7},{4,0},{5,1},{6,2},{7,3},{8,12},{9,13},{10,... | collective-permute-start | bytes 1572872 | tf_op jit(solution)/shard_map/ppermute | solution.py:52
  112.4 14.8 %collective-permute-start.27 = (bf16[2,64,1024]{2,1,0:T(8,128)(2,1)S(1)}, bf16[2,64,1024]{2,1,0:T(8,128)(2,1)S(1)}, u32[]{:S(2)}, u32[]{:S(2)}) collective-permute-start(bf16[2,64,1024]{2,1,0:T(8,128)(2,1)S(1)} %get-tuple-element.13), channel_id=1, source_target_pairs={{0,3},{1,0},{2,1},{3,2},{4,7},{5,4},{6,5},{7,6},{8,11},{9,8},{10,9... | collective-permute-start | bytes 786440 | tf_op jit(solution)/shard_map/ppermute | solution.py:56
  115.7 11.5 %collective-permute-start.26 = (bf16[2,64,1024]{2,1,0:T(8,128)(2,1)S(1)}, bf16[2,64,1024]{2,1,0:T(8,128)(2,1)S(1)}, u32[]{:S(2)}, u32[]{:S(2)}) collective-permute-start(bf16[2,64,1024]{2,1,0:T(8,128)(2,1)S(1)} %get-tuple-element.12), channel_id=1, source_target_pairs={{0,2},{1,3},{2,0},{3,1},{4,6},{5,7},{6,4},{7,5},{8,10},{9,11},{10,... | collective-permute-start | bytes 786440 | tf_op jit(solution)/shard_map/ppermute | solution.py:56
  115.7 14.9 %collective-permute-start.25 = (bf16[2,64,1024]{2,1,0:T(8,128)(2,1)S(1)}, bf16[2,64,1024]{2,1,0:T(8,128)(2,1)S(1)}, u32[]{:S(2)}, u32[]{:S(2)}) collective-permute-start(bf16[2,64,1024]{2,1,0:T(8,128)(2,1)S(1)} %get-tuple-element.11), channel_id=1, source_target_pairs={{0,1},{1,2},{2,3},{3,0},{4,5},{5,6},{6,7},{7,4},{8,9},{9,10},{10,1... | collective-permute-start | bytes 786440 | tf_op jit(solution)/shard_map/ppermute | solution.py:56
  116.7 15.5 %collective-permute-start.33 = (bf16[4,64,1024]{2,1,0:T(8,128)(2,1)S(1)}, bf16[4,64,1024]{2,1,0:T(8,128)(2,1)S(1)}, u32[]{:S(2)}, u32[]{:S(2)}) collective-permute-start(bf16[4,64,1024]{2,1,0:T(8,128)(2,1)S(1)} %fusion.18), channel_id=1, source_target_pairs={{0,4},{1,5},{2,6},{3,7},{4,0},{5,1},{6,2},{7,3},{8,12},{9,13},{10,... | collective-permute-start | bytes 1572872 | tf_op jit(solution)/shard_map/ppermute | solution.py:52
  144.7 9.6 %collective-permute-start.39 = (bf16[64,1024]{1,0:T(8,128)(2,1)S(1)}, bf16[64,1024]{1,0:T(8,128)(2,1)S(1)}, u32[]{:S(2)}, u32[]{:S(2)}) collective-permute-start(bf16[64,1024]{1,0:T(8,128)(2,1)S(1)} %get-tuple-element.61), channel_id=1, source_target_pairs={{0,3},{1,0},{2,1},{3,2},{4,7},{5,4},{6,5},{7,6},{8,11},{9,8},{10,9... | collective-permute-start | bytes 393224 | tf_op jit(solution)/shard_map/ppermute | solution.py:56
  145.8 11.5 %collective-permute-start.37 = (bf16[64,1024]{1,0:T(8,128)(2,1)S(1)}, bf16[64,1024]{1,0:T(8,128)(2,1)S(1)}, u32[]{:S(2)}, u32[]{:S(2)}) collective-permute-start(bf16[64,1024]{1,0:T(8,128)(2,1)S(1)} %get-tuple-element.61), channel_id=1, source_target_pairs={{0,1},{1,2},{2,3},{3,0},{4,5},{5,6},{6,7},{7,4},{8,9},{9,10},{10,1... | collective-permute-start | bytes 393224 | tf_op jit(solution)/shard_map/ppermute | solution.py:56
  147.2 12.9 %collective-permute-start.31 = (bf16[2,64,1024]{2,1,0:T(8,128)(2,1)S(1)}, bf16[2,64,1024]{2,1,0:T(8,128)(2,1)S(1)}, u32[]{:S(2)}, u32[]{:S(2)}) collective-permute-start(bf16[2,64,1024]{2,1,0:T(8,128)(2,1)S(1)} %pad_maximum_fusion.13), channel_id=1, source_target_pairs={{0,2},{1,3},{2,0},{3,1},{4,6},{5,7},{6,4},{7,5},{8,10},{9,11},{10,... | collective-permute-start | bytes 786440 | tf_op jit(solution)/shard_map/ppermute | solution.py:56
  149.5 11.9 %collective-permute-start.32 = (bf16[2,64,1024]{2,1,0:T(8,128)(2,1)S(1)}, bf16[2,64,1024]{2,1,0:T(8,128)(2,1)S(1)}, u32[]{:S(2)}, u32[]{:S(2)}) collective-permute-start(bf16[2,64,1024]{2,1,0:T(8,128)(2,1)S(1)} %pad_maximum_fusion.13), channel_id=1, source_target_pairs={{0,3},{1,0},{2,1},{3,2},{4,7},{5,4},{6,5},{7,6},{8,11},{9,8},{10,9... | collective-permute-start | bytes 786440 | tf_op jit(solution)/shard_map/ppermute | solution.py:56
  151.8 11.2 %collective-permute-start.30 = (bf16[2,64,1024]{2,1,0:T(8,128)(2,1)S(1)}, bf16[2,64,1024]{2,1,0:T(8,128)(2,1)S(1)}, u32[]{:S(2)}, u32[]{:S(2)}) collective-permute-start(bf16[2,64,1024]{2,1,0:T(8,128)(2,1)S(1)} %pad_maximum_fusion.13), channel_id=1, source_target_pairs={{0,1},{1,2},{2,3},{3,0},{4,5},{5,6},{6,7},{7,4},{8,9},{9,10},{10,1... | collective-permute-start | bytes 786440 | tf_op jit(solution)/shard_map/ppermute | solution.py:56
  157.5 9.7 %collective-permute-start.40 = (bf16[4,64,1024]{2,1,0:T(8,128)(2,1)S(1)}, bf16[4,64,1024]{2,1,0:T(8,128)(2,1)S(1)}, u32[]{:S(2)}, u32[]{:S(2)}) collective-permute-start(bf16[4,64,1024]{2,1,0:T(8,128)(2,1)S(1)} %pad_maximum_fusion.10), channel_id=1, source_target_pairs={{0,4},{1,5},{2,6},{3,7},{4,0},{5,1},{6,2},{7,3},{8,12},{9,13},{10,... | collective-permute-start | bytes 1572872 | tf_op jit(solution)/shard_map/ppermute | solution.py:52
  219.4 10.7 %collective-permute-start.52 = (bf16[2,64,1024]{2,1,0:T(8,128)(2,1)S(1)}, bf16[2,64,1024]{2,1,0:T(8,128)(2,1)S(1)}, u32[]{:S(2)}, u32[]{:S(2)}) collective-permute-start(bf16[2,64,1024]{2,1,0:T(8,128)(2,1)S(1)} %get-tuple-element.9), channel_id=1, source_target_pairs={{0,2},{1,3},{2,0},{3,1},{4,6},{5,7},{6,4},{7,5},{8,10},{9,11},{10,... | collective-permute-start | bytes 786440 | tf_op jit(solution)/shard_map/ppermute | solution.py:56
  220.5 14.0 %collective-permute-start.51 = (bf16[2,64,1024]{2,1,0:T(8,128)(2,1)S(1)}, bf16[2,64,1024]{2,1,0:T(8,128)(2,1)S(1)}, u32[]{:S(2)}, u32[]{:S(2)}) collective-permute-start(bf16[2,64,1024]{2,1,0:T(8,128)(2,1)S(1)} %get-tuple-element.8), channel_id=1, source_target_pairs={{0,1},{1,2},{2,3},{3,0},{4,5},{5,6},{6,7},{7,4},{8,9},{9,10},{10,1... | collective-permute-start | bytes 786440 | tf_op jit(solution)/shard_map/ppermute | solution.py:56
  223.3 13.2 %collective-permute-start.55 = (bf16[4,64,1024]{2,1,0:T(8,128)(2,1)S(1)}, bf16[4,64,1024]{2,1,0:T(8,128)(2,1)S(1)}, u32[]{:S(2)}, u32[]{:S(2)}) collective-permute-start(bf16[4,64,1024]{2,1,0:T(8,128)(2,1)S(1)} %fusion.19), channel_id=1, source_target_pairs={{0,4},{1,5},{2,6},{3,7},{4,0},{5,1},{6,2},{7,3},{8,12},{9,13},{10,... | collective-permute-start | bytes 1572872 | tf_op jit(solution)/shard_map/ppermute | solution.py:52
  (52 other events, 369.1 us)

commit v2 on v0

v2 whole, which is shorter than its diff:
```python
import math

import jax
import jax.numpy as jnp
from jax import lax
from jax.experimental import pallas as pl
from jax.experimental.pallas import tpu as pltpu
from jax.sharding import PartitionSpec as P

HALO = 129
EDGE = 144
BLOCK = 256
NBR = 8
ROUNDS = 2
BF16 = jnp.bfloat16
F32 = jnp.float32

PARTS = ((0, 640, (3, 4, 1)), (640, 768, (4, 1, 3)), (1408, 640, (1, 3, 4)))
SAME_X = [[x * 4 + rest for x in range(4)] for rest in range(4)]
VMEM = pl.BlockSpec(memory_space=pltpu.VMEM)
SMEM = pl.BlockSpec(memory_space=pltpu.SMEM)
PARAMS = pltpu.CompilerParams(vmem_limit_bytes=24 * 1024 * 1024)


def hop(a, axis, mask):
    size = lax.axis_size(axis)
    return lax.ppermute(a, axis, [(i, i ^ mask) for i in range(size)])


def hop_x(a, d):
    size = lax.axis_size("pix")
    return lax.ppermute(a, "pix", [(i, (i + 4 * d) % size) for i in range(size)])


def reach(order, position):
    first, second, third = order
    return first * (position // 4) ^ second * (position // 2 % 2) ^ third * (position % 2)


def soften(values, limit):
    return values - jnp.clip(values, -limit, limit)


def nn(a, b):
    return jnp.dot(a, b, preferred_element_type=F32)


def nt(a, b):
    return lax.dot_general(a, b, (((1,), (1,)), ((), ())), preferred_element_type=F32)


def stencil(offsets_ref, movie_ref, before_ref, after_ref, out_ref):
    def band(columns, base):
        step = (
            lax.broadcasted_iota(jnp.int32, (BLOCK, columns), 1)
            - lax.broadcasted_iota(jnp.int32, (BLOCK, columns), 0)
            + base
        )
        weight = jnp.where(step == 0, 1.0, 0.0).astype(F32)
        for k in range(NBR):
            weight = weight - jnp.where(step == offsets_ref[k], 1.0 / NBR, 0.0).astype(F32)
        return weight.astype(BF16)

    rows = movie_ref.shape[0]
    blocks = rows // BLOCK
    main = band(3 * BLOCK, -BLOCK)
    for b in range(blocks):
        low = max(b - 1, 0) * BLOCK
        high = min(b + 2, blocks) * BLOCK
        first = low - (b - 1) * BLOCK
        total = nn(main[:, first : first + high - low], movie_ref[low:high, :])
        if b == 0:
            total += nn(band(EDGE, -EDGE), before_ref[...])
        if b == blocks - 1:
            total += nn(band(EDGE, BLOCK), after_ref[...])
        out_ref[b * BLOCK : (b + 1) * BLOCK, :] = total.astype(BF16)


def contrast(movie, offsets):
    size = lax.axis_size("pix")
    rows = movie.shape[0]
    up = [(i, i + 1) for i in range(size - 1)]
    down = [(j, i) for i, j in up]
    before = lax.ppermute(movie[rows - EDGE :], "pix", up)
    after = lax.ppermute(movie[:EDGE], "pix", down)
    return pl.pallas_call(
        stencil,
        out_shape=jax.ShapeDtypeStruct(movie.shape, BF16),
        in_specs=[SMEM, VMEM, VMEM, VMEM],
        out_specs=VMEM,
        compiler_params=PARAMS,
    )(offsets, movie, before, after)


def place_temporal(place_ref, mine_ref, other_ref, full_ref):
    x, core = place_ref[1], place_ref[2]
    for d in range(4):
        for y in range(2):
            row = (((x + 4 - d) % 4) * 2 + y) * 64
            piece = pl.ds((d * 2 + y) * 32, 32)
            full_ref[pl.ds(pl.multiple_of(row + core * 32, 32), 32), :] = mine_ref[piece, :]
            full_ref[pl.ds(pl.multiple_of(row + 32 - core * 32, 32), 32), :] = other_ref[piece, :]


def temporal_step(
    place_ref, a0, b0, a1, b1, a2, b2, contrasted_ref, mine_ref, other_ref,
    full_ref, send_ref, keep_ref, time_ref, gram_ref, grad_ref,
):
    tm, core = place_ref[0], place_ref[2]
    for (begin, width, order), near, far in zip(PARTS, (a0, a1, a2), (b0, b1, b2)):
        for position in range(8):
            row = pl.multiple_of((tm ^ reach(order, position)) * 64, 64)
            piece = near if position < 4 else far
            full_ref[pl.ds(row, 64), begin : begin + width] = piece[pl.ds(position % 4 * 64, 64), :]
    place_temporal(place_ref, mine_ref, other_ref, time_ref)
    rank, span = time_ref.shape
    scale = 1.0 / math.sqrt(rank)
    for r in range(0, rank, BLOCK):
        gram_ref[r : r + BLOCK, :] = (nt(full_ref[r : r + BLOCK, :], full_ref[...]) * scale).astype(BF16)
    for f in range(0, span, BLOCK):
        columns = slice(f, f + BLOCK)
        grad_ref[...] = nn(full_ref[...], contrasted_ref[:, columns]) - nn(gram_ref[...], time_ref[:, columns])
        for i in range(8):
            piece = pl.ds(i * 32, 32)
            keep_ref[piece, columns] = grad_ref[pl.ds(pl.multiple_of(i * 64 + core * 32, 32), 32), :]
            send_ref[piece, columns] = grad_ref[
                pl.ds(pl.multiple_of(i * 64 + 32 - core * 32, 32), 32), :
            ].astype(BF16)


def spatial_step(
    place_ref, full_ref, contrasted_ref, mine_ref, other_ref,
    s0, k0, s1, k1, s2, k2, time_ref, gram_ref, grad_ref,
):
    tm = place_ref[0]
    place_temporal(place_ref, mine_ref, other_ref, time_ref)
    rank = time_ref.shape[0]
    scale = 1.0 / math.sqrt(rank)
    for r in range(0, rank, BLOCK):
        gram_ref[r : r + BLOCK, :] = (nt(time_ref[r : r + BLOCK, :], time_ref[...]) * scale).astype(BF16)
    for (begin, width, order), send_ref, keep_ref in zip(PARTS, (s0, s1, s2), (k0, k1, k2)):
        for low in range(0, width, BLOCK):
            size = min(BLOCK, width - low)
            pixels = slice(begin + low, begin + low + size)
            columns = slice(low, low + size)
            grad_ref[:, :size] = nt(time_ref[...], contrasted_ref[pixels, :]) - nn(
                gram_ref[...], full_ref[:, pixels]
            )
            for position in range(8):
                row = pl.multiple_of((tm ^ reach(order, position)) * 64, 64)
                piece = grad_ref[pl.ds(row, 64), :size]
                if position < 4:
                    keep_ref[position * 64 : position * 64 + 64, columns] = piece
                else:
                    send_ref[position * 64 - 256 : position * 64 - 192, columns] = piece.astype(BF16)


def per_device(
    movie, offsets, spatial, temporal, step_spatial, step_temporal, thresh_spatial, thresh_temporal
):
    spatial_rows, strip = spatial.shape
    temporal_rows, span = temporal.shape
    rank = spatial_rows * lax.axis_size("tm")
    pixels = strip * lax.axis_size("pix")
    frames = span * lax.axis_size("tm")
    pix = lax.axis_index("pix")
    tm = lax.axis_index("tm")
    x, yhi, core = pix // 4, (pix // 2) % 2, pix % 2
    place = jnp.stack([tm, x, core]).astype(jnp.int32)

    def own(a, index, rows):
        return lax.dynamic_slice_in_dim(a, index * rows, rows, 0)[:, None]

    all_temporal = step_temporal * (math.sqrt(rank) / pixels)
    all_spatial = step_spatial * (math.sqrt(rank) / frames)

    def own_pair(a):
        return jnp.concatenate([own(a, x * 4 + core, temporal_rows), own(a, x * 4 + 2 + core, temporal_rows)])

    def own_slabs(a, mask):
        return jnp.concatenate([own(a, tm, spatial_rows), own(a, tm ^ mask, spatial_rows)])

    coef_temporal, limit_temporal = own_pair(all_temporal), own_pair(thresh_temporal)
    coef_spatial = [own_slabs(all_spatial, order[2]) for _, _, order in PARTS]
    limit_spatial = [own_slabs(thresh_spatial, order[2]) for _, _, order in PARTS]

    def gather_spatial(slabs):
        near = [jnp.concatenate([s, hop(s, "tm", order[1])]) for s, (_, _, order) in zip(slabs, PARTS)]
        return [(a, hop(a, "tm", order[0])) for a, (_, _, order) in zip(near, PARTS)]

    def gather_temporal(pair):
        mine = jnp.concatenate([pair] + [hop_x(pair, d) for d in (1, 2, 3)])
        return mine, hop(mine, "pix", 1)

    shards = [spatial[:, begin : begin + width] for begin, width, _ in PARTS]
    slabs = [jnp.concatenate([s, hop(s, "tm", order[2])]) for s, (_, _, order) in zip(shards, PARTS)]
    pieces = gather_spatial(slabs)
    contrasted = contrast(movie, offsets)
    across = hop(temporal, "pix", 2)
    pair = jnp.concatenate([jnp.where(yhi == 0, temporal, across), jnp.where(yhi == 0, across, temporal)])
    mine, other = gather_temporal(pair)

    for turn in range(ROUNDS):
        full, send, keep = pl.pallas_call(
            temporal_step,
            out_shape=[
                jax.ShapeDtypeStruct((rank, strip), BF16),
                jax.ShapeDtypeStruct((rank // 2, span), BF16),
                jax.ShapeDtypeStruct((rank // 2, span), F32),
            ],
            in_specs=[SMEM] + [VMEM] * 9,
            out_specs=[VMEM] * 3,
            scratch_shapes=[
                pltpu.VMEM((rank, span), BF16),
                pltpu.VMEM((rank, rank), BF16),
                pltpu.VMEM((rank, BLOCK), F32),
            ],
            compiler_params=PARAMS,
        )(place, *[piece for both in pieces for piece in both], contrasted, mine, other)
        grad = (keep + hop(send, "pix", 1).astype(F32)).astype(BF16)
        grad = lax.all_to_all(
            grad.reshape(4, 2 * temporal_rows, span), "pix", 0, 0, axis_index_groups=SAME_X
        )
        grad = jnp.sum(grad.astype(F32), 0).astype(BF16)
        grad = grad.astype(F32) + hop(grad, "pix", 2).astype(F32)
        pair = soften(pair.astype(F32) + coef_temporal * grad, limit_temporal).astype(BF16)
        mine, other = gather_temporal(pair)
        outs = []
        for _, width, _ in PARTS:
            outs += [jax.ShapeDtypeStruct((rank // 2, width), BF16), jax.ShapeDtypeStruct((rank // 2, width), F32)]
        grads = pl.pallas_call(
            spatial_step,
            out_shape=outs,
            in_specs=[SMEM] + [VMEM] * 4,
            out_specs=[VMEM] * 6,
            scratch_shapes=[
                pltpu.VMEM((rank, span), BF16),
                pltpu.VMEM((rank, rank), BF16),
                pltpu.VMEM((rank, BLOCK), F32),
            ],
            compiler_params=PARAMS,
        )(place, full, contrasted, mine, other)
        totals = [
            keep + hop(send, "tm", order[0]).astype(F32)
            for send, keep, (_, _, order) in zip(grads[0::2], grads[1::2], PARTS)
        ]
        half = 2 * spatial_rows
        totals = [
            total[:half] + hop(total[half:].astype(BF16), "tm", order[1]).astype(F32)
            for total, (_, _, order) in zip(totals, PARTS)
        ]
        if turn < ROUNDS - 1:
            sums = []
            for total, (_, _, order) in zip(totals, PARTS):
                mine_sum = total.astype(BF16)
                got = hop(mine_sum, "tm", order[2])
                swapped = jnp.concatenate([got[spatial_rows:], got[:spatial_rows]])
                sums.append(mine_sum.astype(F32) + swapped.astype(F32))
            slabs = [
                soften(s.astype(F32) + coef * g, limit).astype(BF16)
                for s, g, coef, limit in zip(slabs, sums, coef_spatial, limit_spatial)
            ]
            pieces = gather_spatial(slabs)
        else:
            sums = [
                total[:spatial_rows] + hop(total[spatial_rows:].astype(BF16), "tm", order[2]).astype(F32)
                for total, (_, _, order) in zip(totals, PARTS)
            ]
            shards = [
                soften(s[:spatial_rows].astype(F32) + coef[:spatial_rows] * g, limit[:spatial_rows]).astype(BF16)
                for s, g, coef, limit in zip(slabs, sums, coef_spatial, limit_spatial)
            ]
    temporal_out = jnp.where(yhi == 0, pair[:temporal_rows], pair[temporal_rows:])
    return jnp.concatenate(shards, 1), temporal_out


def solution(mesh):
    placed = (P("pix", "tm"), P(), P("tm", "pix"), P("pix", "tm"), P(), P(), P(), P())
    return jax.shard_map(
        per_device,
        mesh=mesh,
        in_specs=placed,
        out_specs=(P("tm", "pix"), P("pix", "tm")),
        check_vma=False,
    )
```

time: 658 us -> 236 us (0.36)
  waiting for transfers between devices: 530 us -> 81 us
  starting transfers between devices: 3.24 us -> 78.8 us
  matrix products: 37.9 us -> 0 us
  Pallas kernels: 0 us -> 25.9 us
  between operations: 24.2 us -> 1.91 us
  other arithmetic: 30.4 us -> 10.8 us
  blocking collectives: 0 us -> 13.3 us
  local copies, waits for them, and re-layouts: 30.4 us -> 20.2 us
    psum x4 -> x0, waiting for transfers between devices: 496 us -> none  [the longest x2 287 us: per_device(): lax.psum(jnp.dot(spatial_full, errors, preferred_element_type=jnp.float32...]
    ppermute x2 -> x52, starting transfers between devices: 2.6 us -> 74.2 us  [the longest x41 57.3 us: hop(): return lax.ppermute(a, axis, [(i, i ^ mask) for i in range(size)])]
    ppermute x2 -> x52, waiting for transfers between devices: 0.01 us -> 71.4 us  [the longest x41 57.8 us: hop(): return lax.ppermute(a, axis, [(i, i ^ mask) for i in range(size)])]
    dot_general x4 -> x0, matrix products: 37.9 us -> none  [the longest x2 19.5 us: per_device(): lax.dot_general(temporal_full, errors, (((1,), (1,)), ((), ())), preferre...]
    all_gather x2 -> x0, waiting for transfers between devices: 32.2 us -> none  [the longest x1 32.1 us: per_device(): spatial_full = lax.all_gather(spatial, 'tm', axis=0, tiled=True)]
    pallas_call x0 -> x5, Pallas kernels: none -> 25.9 us  [the longest x2 10.4 us: per_device(): pl.pallas_call(temporal_step, out_shape=[jax.ShapeDtypeStruct((rank, stri...]
    convert_element_type x5 -> x12, other arithmetic: 30.4 us -> 5.02 us  [the longest x2 2.3 us: per_device(): grad = (keep + hop(send, 'pix', 1).astype(F32)).astype(BF16)]
    concatenate x1, local copies, waits for them, and re-layouts: 24.4 us -> 0.01 us  [gather_temporal(): mine = jnp.concatenate([pair] + [hop_x(pair, d) for d in (1, 2, 3)])]
  transfers between devices with their start and end apart: 8 -> 53, of which waited for: 5 -> 32; matrix products, arithmetic and copies ran while one was open for 8% -> 4% of each run, Pallas kernels for 0% -> 2%
where the time goes in v2:
time: 236 us; the launch traced here: 232 us
  waiting for transfers between devices  81 us (34%)
  starting transfers between devices  78.8 us (33%)
  Pallas kernels  25.9 us (11%)
  local copies, waits for them, and re-layouts  20.2 us (9%)
  blocking collectives  13.3 us (6%)
  other arithmetic  10.8 us (5%)
    ppermute x41, waiting for transfers between devices, hop(): return lax.ppermute(a, axis, [(i, i ^ mask) for i in range(size)])  57.8 us
    ppermute x41, starting transfers between devices, hop(): return lax.ppermute(a, axis, [(i, i ^ mask) for i in range(size)])  57.3 us
    unnamed x84, local copies, waits for them, and re-layouts  16 us
    ppermute x9, starting transfers between devices, hop_x(): lax.ppermute(a, 'pix', [(i, (i + 4 * d) % size) for i in range(size)])  13.5 us
    all_to_all x1, blocking collectives, per_device(): lax.all_to_all(grad.reshape(4, 2 * temporal_rows, span), 'pix', 0, 0, axi...  13.3 us
    ppermute x9, waiting for transfers between devices, hop_x(): lax.ppermute(a, 'pix', [(i, (i + 4 * d) % size) for i in range(size)])  13 us
    pallas_call x2, Pallas kernels, per_device(): pl.pallas_call(temporal_step, out_shape=[jax.ShapeDtypeStruct((rank, stri...  10.4 us
    pallas_call x2, Pallas kernels, per_device(): pl.pallas_call(spatial_step, out_shape=outs, in_specs=[SMEM] + [VMEM] * 4...  10.2 us
  transfers between devices with their start and end apart: 53, of which 32 were waited for; matrix products, arithmetic and copies ran while one was open for 4% of the time, Pallas kernels for 2%

profile of v2, /device:TPU:0, one launch (start us, length us, event | category | flops | bytes accessed | tf_op | source)
XLA Modules:
  0.0 231.7 jit_solution(7631411495616516400)
XLA Ops:
  0.6 3.4 %collective-permute-start.11 = (bf16[32,1024]{1,0:T(8,128)(2,1)}, bf16[32,1024]{1,0:T(8,128)(2,1)S(1)}, u32[]{:S(2)}, u32[]{:S(2)}) collective-permute-start(bf16[32,1024]{1,0:T(8,128)(2,1)} %param.11), channel_id=1, source_target_pairs={{0,16},{8,24},{16,0},{24,8},{32,48},{40,56},{48,32},{56,40},{64,80... | collective-permute-start | bytes 196616 | tf_op jit(solution)/shard_map/ppermute | solution.py:27
  17.7 3.0 %collective-permute-start.13 = (bf16[64,1024]{1,0:T(8,128)(2,1)S(1)}, bf16[64,1024]{1,0:T(8,128)(2,1)S(1)}, u32[]{:S(2)}, u32[]{:S(2)}) collective-permute-start(bf16[64,1024]{1,0:T(8,128)(2,1)S(1)} %pad_maximum_fusion.12), channel_id=1, source_target_pairs={{0,64},{8,72},{16,80},{24,88},{32,96},{40,104},{48,112},{56,120},{... | collective-permute-start | bytes 393224 | tf_op jit(solution)/shard_map/ppermute | solution.py:32
  29.3 5.5 %collective-permute-done.4 = bf16[128,768]{1,0:T(8,128)(2,1)S(1)} collective-permute-done((bf16[128,768]{1,0:T(8,128)(2,1)S(1)}, bf16[128,768]{1,0:T(8,128)(2,1)S(1)}, u32[]{:S(2)}, u32[]{:S(2)}) %collective-permute-start.4) | collective-permute-done | bytes 196640 | tf_op jit(solution)/shard_map/ppermute | solution.py:27
  42.1 5.3 %shard_map.95.contrasted_ref = bf16[2048,1024]{1,0:T(8,128)(2,1)S(1)} custom-call(s32[8]{0:T(128)S(1)} %copy-done.13, bf16[2048,1024]{1,0:T(8,128)(2,1)S(1)} %copy-done.3, bf16[144,1024]{1,0:T(8,128)(2,1)} %collective-permute-done.9.before_ref, bf16[144,1024]{1,0:T(8,128)(2,1)S(1)} %collective-permute-done.10.after_ref), custom_call_target="tpu_custom_call" | custom-call | tf_op jit(solution)/shard_map/pallas_call | solution.py:86
  53.8 5.6 %shard_map.96 = (bf16[512,2048]{1,0:T(8,128)(2,1)S(1)}, bf16[256,1024]{1,0:T(8,128)(2,1)}, f32[256,1024]{1,0:T(8,128)S(1)}) custom-call(s32[3]{0:T(128)S(1)} %pad_add_fusion.place_ref, bf16[256,640]{1,0:T(8,128)(2,1)S(1)} %pad_maximum_fusion.4.a0, bf16[256,640]{1,0:T(8,128)(2,1)S(1)} %copy-done.12, bf16[256,768]{1,0:T(8,128)(2,1)S(1)} %pad_maximum_fusion.2.a1, ...), custom_call_target="tpu_custom_call" | custom-call | tf_op jit(solution)/shard_map/pallas_call | solution.py:204
  62.3 5.8 %collective-permute-start.16 = (bf16[256,1024]{1,0:T(8,128)(2,1)}, bf16[256,1024]{1,0:T(8,128)(2,1)S(1)}, u32[]{:S(2)}, u32[]{:S(2)}) collective-permute-start(bf16[256,1024]{1,0:T(8,128)(2,1)} %get-tuple-element.22), channel_id=1, source_target_pairs={{0,8},{8,0},{16,24},{24,16},{32,40},{40,32},{48,56},{56,48},{64,72... | collective-permute-start | bytes 1572872 | tf_op jit(solution)/shard_map/ppermute | solution.py:27
  72.0 4.5 %all-to-all-start = ((bf16[4,64,1024]{2,1,0:T(8,128)(2,1)}), bf16[4,64,1024]{2,1,0:T(8,128)(2,1)S(1)}, u32[]{:S(2)}, u32[]{:S(2)}) async-start(bf16[4,64,1024]{2,1,0:T(8,128)(2,1)} %bitcast.9), calls=%async_computation | async-start | bytes 1048576 | tf_op jit(solution)/shard_map/all_to_all | solution.py:221
  76.7 9.6 %all-to-all-done = bf16[4,64,1024]{2,1,0:T(8,128)(2,1)S(1)} async-done(((bf16[4,64,1024]{2,1,0:T(8,128)(2,1)}), bf16[4,64,1024]{2,1,0:T(8,128)(2,1)S(1)}, u32[]{:S(2)}, u32[]{:S(2)}) %all-to-all-start) | async-done | bytes 524320 | tf_op jit(solution)/shard_map/all_to_all | solution.py:221
  86.4 3.5 %collective-permute-start.17 = (bf16[64,1024]{1,0:T(8,128)(2,1)S(1)}, bf16[64,1024]{1,0:T(8,128)(2,1)S(1)}, u32[]{:S(2)}, u32[]{:S(2)}) collective-permute-start(bf16[64,1024]{1,0:T(8,128)(2,1)S(1)} %reduce_sum.24), channel_id=1, source_target_pairs={{0,16},{8,24},{16,0},{24,8},{32,48},{40,56},{48,32},{56,40},{64,80... | collective-permute-start | bytes 393224 | tf_op jit(solution)/shard_map/ppermute | solution.py:27
  97.4 4.4 %collective-permute-done.18 = bf16[64,1024]{1,0:T(8,128)(2,1)S(1)} collective-permute-done((bf16[64,1024]{1,0:T(8,128)(2,1)S(1)}, bf16[64,1024]{1,0:T(8,128)(2,1)S(1)}, u32[]{:S(2)}, u32[]{:S(2)}) %collective-permute-start.18) | collective-permute-done | bytes 131104 | tf_op jit(solution)/shard_map/ppermute | solution.py:32
  107.2 5.1 %shard_map.97 = (bf16[256,640]{1,0:T(8,128)(2,1)S(1)}, f32[256,640]{1,0:T(8,128)S(1)}, bf16[256,768]{1,0:T(8,128)(2,1)S(1)}, f32[256,768]{1,0:T(8,128)S(1)}, bf1...) custom-call(s32[3]{0:T(128)S(1)} %pad_add_fusion.place_ref, bf16[512,2048]{1,0:T(8,128)(2,1)S(1)} %get-tuple-element.20.full_ref, ...), custom_call_target="tpu_custom_call" | custom-call | tf_op jit(solution)/shard_map/pallas_call | solution.py:231
  115.7 6.8 %collective-permute-done.32 = bf16[256,640]{1,0:T(8,128)(2,1)S(1)} collective-permute-done((bf16[256,640]{1,0:T(8,128)(2,1)S(1)}, bf16[256,640]{1,0:T(8,128)(2,1)S(1)}, u32[]{:S(2)}, u32[]{:S(2)}) %collective-permute-start.32) | collective-permute-done | bytes 327712 | tf_op jit(solution)/shard_map/ppermute | solution.py:27
  138.0 3.0 %collective-permute-done.29 = bf16[128,768]{1,0:T(8,128)(2,1)S(1)} collective-permute-done((bf16[128,768]{1,0:T(8,128)(2,1)S(1)}, bf16[128,768]{1,0:T(8,128)(2,1)S(1)}, u32[]{:S(2)}, u32[]{:S(2)}) %collective-permute-start.29) | collective-permute-done | bytes 196640 | tf_op jit(solution)/shard_map/ppermute | solution.py:27
  144.4 4.0 %collective-permute-done.30 = bf16[128,768]{1,0:T(8,128)(2,1)S(1)} collective-permute-done((bf16[128,768]{1,0:T(8,128)(2,1)S(1)}, bf16[128,768]{1,0:T(8,128)(2,1)S(1)}, u32[]{:S(2)}, u32[]{:S(2)}) %collective-permute-start.30) | collective-permute-done | bytes 196640 | tf_op jit(solution)/shard_map/ppermute | solution.py:27
  148.7 3.4 %collective-permute-start.26 = (bf16[256,640]{1,0:T(8,128)(2,1)S(1)}, bf16[256,640]{1,0:T(8,128)(2,1)S(1)}, u32[]{:S(2)}, u32[]{:S(2)}) collective-permute-start(bf16[256,640]{1,0:T(8,128)(2,1)S(1)} %pad_maximum_fusion.6.a0), channel_id=1, source_target_pairs={{0,3},{1,2},{2,1},{3,0},{4,7},{5,6},{6,5},{7,4},{8,11},{9,10},{10,... | collective-permute-start | bytes 983048 | tf_op jit(solution)/shard_map/ppermute | solution.py:27
  152.1 5.3 %collective-permute-done.26.b0 = bf16[256,640]{1,0:T(8,128)(2,1)S(1)} collective-permute-done((bf16[256,640]{1,0:T(8,128)(2,1)S(1)}, bf16[256,640]{1,0:T(8,128)(2,1)S(1)}, u32[]{:S(2)}, u32[]{:S(2)}) %collective-permute-start.26) | collective-permute-done | bytes 327712 | tf_op jit(solution)/shard_map/ppermute | solution.py:27
  157.4 4.8 %shard_map.98 = (bf16[512,2048]{1,0:T(8,128)(2,1)S(1)}, bf16[256,1024]{1,0:T(8,128)(2,1)S(1)}, f32[256,1024]{1,0:T(8,128)S(1)}) custom-call(s32[3]{0:T(128)S(1)} %pad_add_fusion.place_ref, bf16[256,640]{1,0:T(8,128)(2,1)S(1)} %pad_maximum_fusion.6.a0, bf16[256,640]{1,0:T(8,128)(2,1)S(1)} %collective-permute-done.26.b0, ...), custom_call_target="tpu_custom_call" | custom-call | tf_op jit(solution)/shard_map/pallas_call | solution.py:204
  164.3 13.3 %all_to_all.10 = bf16[4,64,1024]{2,1,0:T(8,128)(2,1)S(1)} all-to-all(bf16[4,64,1024]{2,1,0:T(8,128)(2,1)S(1)} %bitcast.38), channel_id=1, replica_groups={{0,32,64,96},{8,40,72,104},{16,48,80,112},{24,56,88,120},{1,33,65,97},{..., dimensions={0} | all-to-all | bytes 1048576 | tf_op jit(solution)/shard_map/all_to_all | solution.py:221
  177.7 4.6 %collective-permute-start.38 = (bf16[64,1024]{1,0:T(8,128)(2,1)S(1)}, bf16[64,1024]{1,0:T(8,128)(2,1)S(1)}, u32[]{:S(2)}, u32[]{:S(2)}) collective-permute-start(bf16[64,1024]{1,0:T(8,128)(2,1)S(1)} %reduce_sum.25), channel_id=1, source_target_pairs={{0,16},{8,24},{16,0},{24,8},{32,48},{40,56},{48,32},{56,40},{64,80... | collective-permute-start | bytes 393224 | tf_op jit(solution)/shard_map/ppermute | solution.py:27
  182.2 2.9 %collective-permute-done.38 = bf16[64,1024]{1,0:T(8,128)(2,1)S(1)} collective-permute-done((bf16[64,1024]{1,0:T(8,128)(2,1)S(1)}, bf16[64,1024]{1,0:T(8,128)(2,1)S(1)}, u32[]{:S(2)}, u32[]{:S(2)}) %collective-permute-start.38) | collective-permute-done | bytes 131104 | tf_op jit(solution)/shard_map/ppermute | solution.py:27
  189.5 4.1 %collective-permute-done.39 = bf16[64,1024]{1,0:T(8,128)(2,1)S(1)} collective-permute-done((bf16[64,1024]{1,0:T(8,128)(2,1)S(1)}, bf16[64,1024]{1,0:T(8,128)(2,1)S(1)}, u32[]{:S(2)}, u32[]{:S(2)}) %collective-permute-start.39) | collective-permute-done | bytes 131104 | tf_op jit(solution)/shard_map/ppermute | solution.py:32
  198.7 5.1 %shard_map.99 = (bf16[256,640]{1,0:T(8,128)(2,1)S(1)}, f32[256,640]{1,0:T(8,128)S(1)}, bf16[256,768]{1,0:T(8,128)(2,1)S(1)}, f32[256,768]{1,0:T(8,128)S(1)}, bf1...) custom-call(s32[3]{0:T(128)S(1)} %pad_add_fusion.place_ref, bf16[512,2048]{1,0:T(8,128)(2,1)S(1)} %get-tuple-element.29.full_ref, ...), custom_call_target="tpu_custom_call" | custom-call | tf_op jit(solution)/shard_map/pallas_call | solution.py:231
  207.6 6.1 %collective-permute-done.49 = bf16[256,640]{1,0:T(8,128)(2,1)S(1)} collective-permute-done((bf16[256,640]{1,0:T(8,128)(2,1)S(1)}, bf16[256,640]{1,0:T(8,128)(2,1)S(1)}, u32[]{:S(2)}, u32[]{:S(2)}) %collective-permute-start.49) | collective-permute-done | bytes 327712 | tf_op jit(solution)/shard_map/ppermute | solution.py:27
  226.3 4.1 %collective-permute-done.48 = bf16[64,768]{1,0:T(8,128)(2,1)S(1)} collective-permute-done((bf16[64,768]{1,0:T(8,128)(2,1)S(1)}, bf16[64,768]{1,0:T(8,128)(2,1)S(1)}, u32[]{:S(2)}, u32[]{:S(2)}) %collective-permute-start.48) | collective-permute-done | bytes 98336 | tf_op jit(solution)/shard_map/ppermute | solution.py:27
  (238 shorter events, 106.7 us)
Async XLA Ops:
  0.6 13.8 %collective-permute-start.11 = (bf16[32,1024]{1,0:T(8,128)(2,1)}, bf16[32,1024]{1,0:T(8,128)(2,1)S(1)}, u32[]{:S(2)}, u32[]{:S(2)}) collective-permute-start(bf16[32,1024]{1,0:T(8,128)(2,1)} %param.11), channel_id=1, source_target_pairs={{0,16},{8,24},{16,0},{24,8},{32,48},{40,56},{48,32},{56,40},{64,80... | collective-permute-start | bytes 196616 | tf_op jit(solution)/shard_map/ppermute | solution.py:27
  5.0 12.7 %collective-permute-start.6 = (bf16[64,640]{1,0:T(8,128)(2,1)S(1)}, bf16[64,640]{1,0:T(8,128)(2,1)S(1)}, u32[]{:S(2)}, u32[]{:S(2)}) collective-permute-start(bf16[64,640]{1,0:T(8,128)(2,1)S(1)} %get-tuple-element.46), channel_id=1, source_target_pairs={{0,4},{1,5},{2,6},{3,7},{4,0},{5,1},{6,2},{7,3},{8,12},{9,13},{10,... | collective-permute-start | bytes 245768 | tf_op jit(solution)/shard_map/ppermute | solution.py:27
  5.7 15.0 %collective-permute-start = (bf16[64,640]{1,0:T(8,128)(2,1)S(1)}, bf16[64,640]{1,0:T(8,128)(2,1)S(1)}, u32[]{:S(2)}, u32[]{:S(2)}) collective-permute-start(bf16[64,640]{1,0:T(8,128)(2,1)S(1)} %get-tuple-element.47), channel_id=1, source_target_pairs={{0,1},{1,0},{2,3},{3,2},{4,5},{5,4},{6,7},{7,6},{8,9},{9,8},{10,11... | collective-permute-start | bytes 245768 | tf_op jit(solution)/shard_map/ppermute | solution.py:27
  8.5 13.4 %collective-permute-start.3 = (bf16[64,768]{1,0:T(8,128)(2,1)S(1)}, bf16[64,768]{1,0:T(8,128)(2,1)S(1)}, u32[]{:S(2)}, u32[]{:S(2)}) collective-permute-start(bf16[64,768]{1,0:T(8,128)(2,1)S(1)} %slice.112), channel_id=1, source_target_pairs={{0,3},{1,2},{2,1},{3,0},{4,7},{5,6},{6,5},{7,4},{8,11},{9,10},{10,... | collective-permute-start | bytes 294920 | tf_op jit(solution)/shard_map/ppermute | solution.py:27
  13.1 24.0 %collective-permute-start.10 = (bf16[144,1024]{1,0:T(8,128)(2,1)}, bf16[144,1024]{1,0:T(8,128)(2,1)S(1)}, u32[]{:S(2)}, u32[]{:S(2)}) collective-permute-start(bf16[144,1024]{1,0:T(8,128)(2,1)} %get-tuple-element.44), channel_id=1, source_target_pairs={{8,0},{16,8},{24,16},{32,24},{40,32},{48,40},{56,48},{64,56},{72,6... | collective-permute-start | bytes 884744 | tf_op jit(solution)/shard_map/ppermute | solution.py:85
  15.4 7.8 %collective-permute-start.12 = (bf16[64,1024]{1,0:T(8,128)(2,1)S(1)}, bf16[64,1024]{1,0:T(8,128)(2,1)S(1)}, u32[]{:S(2)}, u32[]{:S(2)}) collective-permute-start(bf16[64,1024]{1,0:T(8,128)(2,1)S(1)} %pad_maximum_fusion.12), channel_id=1, source_target_pairs={{0,32},{8,40},{16,48},{24,56},{32,64},{40,72},{48,80},{56,88},{64,... | collective-permute-start | bytes 393224 | tf_op jit(solution)/shard_map/ppermute | solution.py:32
  17.7 9.3 %collective-permute-start.13 = (bf16[64,1024]{1,0:T(8,128)(2,1)S(1)}, bf16[64,1024]{1,0:T(8,128)(2,1)S(1)}, u32[]{:S(2)}, u32[]{:S(2)}) collective-permute-start(bf16[64,1024]{1,0:T(8,128)(2,1)S(1)} %pad_maximum_fusion.12), channel_id=1, source_target_pairs={{0,64},{8,72},{16,80},{24,88},{32,96},{40,104},{48,112},{56,120},{... | collective-permute-start | bytes 393224 | tf_op jit(solution)/shard_map/ppermute | solution.py:32
  23.2 13.1 %collective-permute-start.1 = (bf16[128,640]{1,0:T(8,128)(2,1)S(1)}, bf16[128,640]{1,0:T(8,128)(2,1)S(1)}, u32[]{:S(2)}, u32[]{:S(2)}) collective-permute-start(bf16[128,640]{1,0:T(8,128)(2,1)S(1)} %pad_maximum_fusion.10), channel_id=1, source_target_pairs={{0,4},{1,5},{2,6},{3,7},{4,0},{5,1},{6,2},{7,3},{8,12},{9,13},{10,... | collective-permute-start | bytes 491528 | tf_op jit(solution)/shard_map/ppermute | solution.py:27
  28.0 20.9 %collective-permute-start.15 = (bf16[256,1024]{1,0:T(8,128)(2,1)S(1)}, bf16[256,1024]{1,0:T(8,128)(2,1)S(1)}, u32[]{:S(2)}, u32[]{:S(2)}) collective-permute-start(bf16[256,1024]{1,0:T(8,128)(2,1)S(1)} %constant_dynamic-update-slice_fusion.mine_ref), channel_id=1, source_target_pairs={{0,8},{8,0},{16,24},{24,16},{32,40},{40,32},{48,56},{56,48},{64,72... | collective-permute-start | bytes 1572872 | tf_op jit(solution)/shard_map/ppermute | solution.py:27
  29.0 18.5 %collective-permute-start.8 = (bf16[256,640]{1,0:T(8,128)(2,1)S(1)}, bf16[256,640]{1,0:T(8,128)(2,1)S(1)}, u32[]{:S(2)}, u32[]{:S(2)}) collective-permute-start(bf16[256,640]{1,0:T(8,128)(2,1)S(1)} %pad_maximum_fusion.5.a2), channel_id=1, source_target_pairs={{0,1},{1,0},{2,3},{3,2},{4,5},{5,4},{6,7},{7,6},{8,9},{9,8},{10,11... | collective-permute-start | bytes 983048 | tf_op jit(solution)/shard_map/ppermute | solution.py:27
  34.8 14.2 %collective-permute-start.5 = (bf16[256,768]{1,0:T(8,128)(2,1)S(1)}, bf16[256,768]{1,0:T(8,128)(2,1)S(1)}, u32[]{:S(2)}, u32[]{:S(2)}) collective-permute-start(bf16[256,768]{1,0:T(8,128)(2,1)S(1)} %pad_maximum_fusion.2.a1), channel_id=1, source_target_pairs={{0,4},{1,5},{2,6},{3,7},{4,0},{5,1},{6,2},{7,3},{8,12},{9,13},{10,... | collective-permute-start | bytes 1179656 | tf_op jit(solution)/shard_map/ppermute | solution.py:27
  36.3 11.8 %collective-permute-start.2 = (bf16[256,640]{1,0:T(8,128)(2,1)S(1)}, bf16[256,640]{1,0:T(8,128)(2,1)S(1)}, u32[]{:S(2)}, u32[]{:S(2)}) collective-permute-start(bf16[256,640]{1,0:T(8,128)(2,1)S(1)} %pad_maximum_fusion.4.a0), channel_id=1, source_target_pairs={{0,3},{1,2},{2,1},{3,0},{4,7},{5,6},{6,5},{7,4},{8,11},{9,10},{10,... | collective-permute-start | bytes 983048 | tf_op jit(solution)/shard_map/ppermute | solution.py:27
  72.0 14.3 %all-to-all-start = ((bf16[4,64,1024]{2,1,0:T(8,128)(2,1)}), bf16[4,64,1024]{2,1,0:T(8,128)(2,1)S(1)}, u32[]{:S(2)}, u32[]{:S(2)}) async-start(bf16[4,64,1024]{2,1,0:T(8,128)(2,1)} %bitcast.9), calls=%async_computation | async-start | bytes 1048576 | tf_op jit(solution)/shard_map/all_to_all | solution.py:221
  94.0 7.8 %collective-permute-start.18 = (bf16[64,1024]{1,0:T(8,128)(2,1)S(1)}, bf16[64,1024]{1,0:T(8,128)(2,1)S(1)}, u32[]{:S(2)}, u32[]{:S(2)}) collective-permute-start(bf16[64,1024]{1,0:T(8,128)(2,1)S(1)} %subtract_convert_fusion.4), channel_id=1, source_target_pairs={{0,32},{8,40},{16,48},{24,56},{32,64},{40,72},{48,80},{56,88},{64,... | collective-permute-start | bytes 393224 | tf_op jit(solution)/shard_map/ppermute | solution.py:32
  112.3 10.2 %collective-permute-start.32 = (bf16[256,640]{1,0:T(8,128)(2,1)S(1)}, bf16[256,640]{1,0:T(8,128)(2,1)S(1)}, u32[]{:S(2)}, u32[]{:S(2)}) collective-permute-start(bf16[256,640]{1,0:T(8,128)(2,1)S(1)} %get-tuple-element.28), channel_id=1, source_target_pairs={{0,1},{1,0},{2,3},{3,2},{4,5},{5,4},{6,7},{7,6},{8,9},{9,8},{10,11... | collective-permute-start | bytes 983048 | tf_op jit(solution)/shard_map/ppermute | solution.py:27
  113.5 11.7 %collective-permute-start.22 = (bf16[256,640]{1,0:T(8,128)(2,1)S(1)}, bf16[256,640]{1,0:T(8,128)(2,1)S(1)}, u32[]{:S(2)}, u32[]{:S(2)}) collective-permute-start(bf16[256,640]{1,0:T(8,128)(2,1)S(1)} %get-tuple-element.24), channel_id=1, source_target_pairs={{0,3},{1,2},{2,1},{3,0},{4,7},{5,6},{6,5},{7,4},{8,11},{9,10},{10,... | collective-permute-start | bytes 983048 | tf_op jit(solution)/shard_map/ppermute | solution.py:27
  115.6 10.9 %collective-permute-start.27 = (bf16[256,768]{1,0:T(8,128)(2,1)S(1)}, bf16[256,768]{1,0:T(8,128)(2,1)S(1)}, u32[]{:S(2)}, u32[]{:S(2)}) collective-permute-start(bf16[256,768]{1,0:T(8,128)(2,1)S(1)} %get-tuple-element.26), channel_id=1, source_target_pairs={{0,4},{1,5},{2,6},{3,7},{4,0},{5,1},{6,2},{7,3},{8,12},{9,13},{10,... | collective-permute-start | bytes 1179656 | tf_op jit(solution)/shard_map/ppermute | solution.py:27
  133.0 8.0 %collective-permute-start.29 = (bf16[128,768]{1,0:T(8,128)(2,1)S(1)}, bf16[128,768]{1,0:T(8,128)(2,1)S(1)}, u32[]{:S(2)}, u32[]{:S(2)}) collective-permute-start(bf16[128,768]{1,0:T(8,128)(2,1)S(1)} %fusion), channel_id=1, source_target_pairs={{0,3},{1,2},{2,1},{3,0},{4,7},{5,6},{6,5},{7,4},{8,11},{9,10},{10,... | collective-permute-start | bytes 589832 | tf_op jit(solution)/shard_map/ppermute | solution.py:27
  142.8 9.3 %collective-permute-start.36 = (bf16[256,640]{1,0:T(8,128)(2,1)S(1)}, bf16[256,640]{1,0:T(8,128)(2,1)S(1)}, u32[]{:S(2)}, u32[]{:S(2)}) collective-permute-start(bf16[256,640]{1,0:T(8,128)(2,1)S(1)} %pad_maximum_fusion.7.a2), channel_id=1, source_target_pairs={{0,1},{1,0},{2,3},{3,2},{4,5},{5,4},{6,7},{7,6},{8,9},{9,8},{10,11... | collective-permute-start | bytes 983048 | tf_op jit(solution)/shard_map/ppermute | solution.py:27
  148.4 8.9 %collective-permute-start.31 = (bf16[256,768]{1,0:T(8,128)(2,1)S(1)}, bf16[256,768]{1,0:T(8,128)(2,1)S(1)}, u32[]{:S(2)}, u32[]{:S(2)}) collective-permute-start(bf16[256,768]{1,0:T(8,128)(2,1)S(1)} %pad_maximum_fusion.3.a1), channel_id=1, source_target_pairs={{0,4},{1,5},{2,6},{3,7},{4,0},{5,1},{6,2},{7,3},{8,12},{9,13},{10,... | collective-permute-start | bytes 1179656 | tf_op jit(solution)/shard_map/ppermute | solution.py:27
  148.7 8.6 %collective-permute-start.26 = (bf16[256,640]{1,0:T(8,128)(2,1)S(1)}, bf16[256,640]{1,0:T(8,128)(2,1)S(1)}, u32[]{:S(2)}, u32[]{:S(2)}) collective-permute-start(bf16[256,640]{1,0:T(8,128)(2,1)S(1)} %pad_maximum_fusion.6.a0), channel_id=1, source_target_pairs={{0,3},{1,2},{2,1},{3,0},{4,7},{5,6},{6,5},{7,4},{8,11},{9,10},{10,... | collective-permute-start | bytes 983048 | tf_op jit(solution)/shard_map/ppermute | solution.py:27
  203.9 9.8 %collective-permute-start.49 = (bf16[256,640]{1,0:T(8,128)(2,1)S(1)}, bf16[256,640]{1,0:T(8,128)(2,1)S(1)}, u32[]{:S(2)}, u32[]{:S(2)}) collective-permute-start(bf16[256,640]{1,0:T(8,128)(2,1)S(1)} %get-tuple-element.37), channel_id=1, source_target_pairs={{0,1},{1,0},{2,3},{3,2},{4,5},{5,4},{6,7},{7,6},{8,9},{9,8},{10,11... | collective-permute-start | bytes 983048 | tf_op jit(solution)/shard_map/ppermute | solution.py:27
  204.0 12.0 %collective-permute-start.43 = (bf16[256,640]{1,0:T(8,128)(2,1)S(1)}, bf16[256,640]{1,0:T(8,128)(2,1)S(1)}, u32[]{:S(2)}, u32[]{:S(2)}) collective-permute-start(bf16[256,640]{1,0:T(8,128)(2,1)S(1)} %get-tuple-element.33), channel_id=1, source_target_pairs={{0,3},{1,2},{2,1},{3,0},{4,7},{5,6},{6,5},{7,4},{8,11},{9,10},{10,... | collective-permute-start | bytes 983048 | tf_op jit(solution)/shard_map/ppermute | solution.py:27
  206.7 10.9 %collective-permute-start.46 = (bf16[256,768]{1,0:T(8,128)(2,1)S(1)}, bf16[256,768]{1,0:T(8,128)(2,1)S(1)}, u32[]{:S(2)}, u32[]{:S(2)}) collective-permute-start(bf16[256,768]{1,0:T(8,128)(2,1)S(1)} %get-tuple-element.35), channel_id=1, source_target_pairs={{0,4},{1,5},{2,6},{3,7},{4,0},{5,1},{6,2},{7,3},{8,12},{9,13},{10,... | collective-permute-start | bytes 1179656 | tf_op jit(solution)/shard_map/ppermute | solution.py:27
  (70 other events, 775.3 us)

commit v3 on v2

v3 whole, which is shorter than its diff:
```python
import functools
import math

import jax
import jax.numpy as jnp
from jax import lax
from jax.experimental import pallas as pl
from jax.experimental.pallas import tpu as pltpu
from jax.sharding import PartitionSpec as P

HALO = 129
EDGE = 144
BLOCK = 256
NBR = 8
ROUNDS = 2
BF16 = jnp.bfloat16
F32 = jnp.float32

PARTS = ((0, 640, (3, 4, 1)), (640, 768, (4, 1, 3)), (1408, 640, (1, 3, 4)))
VMEM = pl.BlockSpec(memory_space=pltpu.VMEM)
SMEM = pl.BlockSpec(memory_space=pltpu.SMEM)
ANY = pl.BlockSpec(memory_space=pl.ANY)
HBM = pl.BlockSpec(memory_space=pltpu.HBM)
COPIES = pltpu.SemaphoreType.DMA((64,))
PARAMS = pltpu.CompilerParams(vmem_limit_bytes=20 * 1024 * 1024)


def hop(a, axis, mask):
    size = lax.axis_size(axis)
    return lax.ppermute(a, axis, [(i, i ^ mask) for i in range(size)])


def hop_x(a, second):
    size = lax.axis_size("pix")
    return lax.ppermute(a, "pix", [(i, i ^ 4 * (1 if i % 2 == second else 3)) for i in range(size)])


def reach(order, position):
    first, second, third = order
    return first * (position // 4) ^ second * (position // 2 % 2) ^ third * (position % 2)


def soften(values, limit):
    return values - jnp.clip(values, -limit, limit)


def nn(a, b):
    return jnp.dot(a, b, preferred_element_type=F32)


def nt(a, b):
    return lax.dot_general(a, b, (((1,), (1,)), ((), ())), preferred_element_type=F32)


class Copies:
    def __init__(self, sems):
        self.sems = sems
        self.used = 0

    def start(self, source, target):
        copy = pltpu.make_async_copy(source, target, self.sems.at[self.used])
        self.used += 1
        copy.start()
        return copy


def stencil(offsets_ref, movie_ref, before_ref, after_ref, later_ref, out_ref, held_ref, made_ref, sems):
    del later_ref
    rows = movie_ref.shape[0]
    blocks = rows // BLOCK
    copies = Copies(sems)

    def block(b):
        return pl.ds(b * BLOCK, BLOCK)

    loads = [copies.start(movie_ref.at[block(b), :], held_ref.at[block(b), :]) for b in range(blocks)]

    def band(columns, base):
        step = (
            lax.broadcasted_iota(jnp.int32, (BLOCK, columns), 1)
            - lax.broadcasted_iota(jnp.int32, (BLOCK, columns), 0)
            + base
        )
        weight = jnp.where(step == 0, 1.0, 0.0).astype(F32)
        for k in range(NBR):
            weight = weight - jnp.where(step == offsets_ref[k], 1.0 / NBR, 0.0).astype(F32)
        return weight.astype(BF16)

    main = band(3 * BLOCK, -BLOCK)
    loads[0].wait()
    stores = []
    for b in range(blocks):
        if b + 1 < blocks:
            loads[b + 1].wait()
        low = max(b - 1, 0) * BLOCK
        high = min(b + 2, blocks) * BLOCK
        first = low - (b - 1) * BLOCK
        total = nn(main[:, first : first + high - low], held_ref[low:high, :])
        if b == 0:
            total += nn(band(EDGE, -EDGE), before_ref[...])
        if b == blocks - 1:
            total += nn(band(EDGE, BLOCK), after_ref[...])
        made_ref[b * BLOCK : (b + 1) * BLOCK, :] = total.astype(BF16)
        stores.append(copies.start(made_ref.at[block(b), :], out_ref.at[block(b), :]))
    for store in stores:
        store.wait()


def contrast(movie, before, after, offsets, later):
    return pl.pallas_call(
        stencil,
        out_shape=pltpu.HBM(movie.shape, BF16),
        in_specs=[SMEM, HBM, VMEM, VMEM, ANY],
        out_specs=HBM,
        scratch_shapes=[pltpu.VMEM(movie.shape, BF16), pltpu.VMEM(movie.shape, BF16), COPIES],
        compiler_params=PARAMS,
    )(offsets, in_hbm(movie), before, after, later)


def in_hbm(a):
    return pltpu.with_memory_space_constraint(a, pltpu.HBM)


def row_of(x, y, core):
    return pl.multiple_of((x * 2 + y) * 64 + core * 32, 32)


def near_x(x, core, position):
    first, second = 1 + 2 * core, 3 - 2 * core
    return x ^ (first * (position // 2)) ^ (second * (position % 2))


def temporal_rows(place_ref, source_ref, target_ref, flip):
    x, core = place_ref[1], place_ref[2] ^ flip
    for position in range(4):
        for y in range(2):
            piece = pl.ds(position * 64 + y * 32, 32)
            target_ref[piece, :] = source_ref[pl.ds(row_of(near_x(x, core, position), y, core), 32), :]


def place_temporal(place_ref, mine_ref, other_ref, time_ref, copies):
    x, core = place_ref[1], place_ref[2]
    loads = []
    for position in range(4):
        for y in range(2):
            piece = pl.ds(position * 64 + y * 32, 32)
            for from_ref, side in ((mine_ref, core), (other_ref, core ^ 1)):
                row = row_of(near_x(x, side, position), y, side)
                loads.append(copies.start(from_ref.at[piece, :], time_ref.at[pl.ds(row, 32), :]))
    return loads


def temporal_send(
    place_ref, a0, b0, a1, b1, a2, b2, contrasted_ref, mine_ref, other_ref,
    full_ref, time_ref, stored_ref, send_ref, rows_ref, gram_ref, held_ref, sems,
):
    tm = place_ref[0]
    copies = Copies(sems)
    loads = []
    for (begin, width, order), near, far in zip(PARTS, (a0, a1, a2), (b0, b1, b2)):
        for position in range(8):
            row = pl.multiple_of((tm ^ reach(order, position)) * 64, 64)
            piece = near if position < 4 else far
            loads.append(
                copies.start(
                    piece.at[pl.ds(position % 4 * 64, 64), :],
                    full_ref.at[pl.ds(row, 64), pl.ds(begin, width)],
                )
            )
    blocks = hold(contrasted_ref, held_ref, copies)
    times = place_temporal(place_ref, mine_ref, other_ref, time_ref, copies)
    for load in loads:
        load.wait()
    store = copies.start(full_ref, stored_ref)
    temporal_half(place_ref, full_ref, time_ref, send_ref, rows_ref, gram_ref, held_ref, blocks, times, 1)
    store.wait()


def temporal_keep(
    place_ref, full_ref, contrasted_ref, time_ref, keep_ref, rows_ref, gram_ref, held_ref, sems
):
    blocks = hold(contrasted_ref, held_ref, Copies(sems))
    temporal_half(place_ref, full_ref, time_ref, keep_ref, rows_ref, gram_ref, held_ref, blocks, [], 0)


def hold(contrasted_ref, held_ref, copies):
    span = held_ref.shape[1]
    return [
        copies.start(contrasted_ref.at[:, pl.ds(f, BLOCK)], held_ref.at[:, pl.ds(f, BLOCK)])
        for f in range(0, span, BLOCK)
    ]


def temporal_half(
    place_ref, full_ref, time_ref, out_ref, rows_ref, gram_ref, held_ref, blocks, times, flip
):
    temporal_rows(place_ref, full_ref, rows_ref, flip)
    rank, span = time_ref.shape
    gram_ref[...] = (nt(rows_ref[...], full_ref[...]) * (1.0 / math.sqrt(rank))).astype(BF16)
    for load in times:
        load.wait()
    for f in range(0, span, BLOCK):
        columns = slice(f, f + BLOCK)
        blocks[f // BLOCK].wait()
        grad = nn(rows_ref[...], held_ref[:, columns]) - nn(gram_ref[...], time_ref[:, columns])
        out_ref[:, columns] = grad.astype(out_ref.dtype)


def spatial_loads(part, full_ref, contrasted_ref, strip_ref, held_ref, copies):
    begin, width, _ = PARTS[part]
    return [
        copies.start(contrasted_ref.at[pl.ds(begin, width), :], held_ref.at[pl.ds(0, width), :]),
        copies.start(full_ref.at[:, pl.ds(begin, width)], strip_ref.at[:, pl.ds(0, width)]),
    ]


def spatial_half(
    part, place_ref, time_ref, gram_ref, send_ref, keep_ref, rows_ref, weight_ref, strip_ref, held_ref, loads
):
    _, width, order = PARTS[part]
    tm = place_ref[0]
    for position in range(8):
        row = pl.multiple_of((tm ^ reach(order, position)) * 64, 64)
        piece = pl.ds(position * 64, 64)
        rows_ref[piece, :] = time_ref[pl.ds(row, 64), :]
        weight_ref[piece, :] = gram_ref[pl.ds(row, 64), :]
    for load in loads:
        load.wait()
    half = rows_ref.shape[0] // 2
    for low in range(0, width, BLOCK):
        size = min(BLOCK, width - low)
        pixels = slice(low, low + size)
        for out_ref, first in ((send_ref, half), (keep_ref, 0)):
            rows = slice(first, first + half)
            grad = nt(rows_ref[rows, :], held_ref[pixels, :]) - nn(weight_ref[rows, :], strip_ref[:, pixels])
            out_ref[:, pixels] = grad.astype(out_ref.dtype)


def spatial_part(
    part, place_ref, full_ref, contrasted_ref, time_ref, gram_ref,
    send_ref, keep_ref, rows_ref, weight_ref, strip_ref, held_ref, sems,
):
    loads = spatial_loads(part, full_ref, contrasted_ref, strip_ref, held_ref, Copies(sems))
    spatial_half(
        part, place_ref, time_ref, gram_ref, send_ref, keep_ref, rows_ref, weight_ref, strip_ref, held_ref, loads
    )


def spatial_first(
    place_ref, full_ref, contrasted_ref, mine_ref, other_ref,
    send_ref, keep_ref, time_ref, gram_ref, rows_ref, weight_ref, strip_ref, held_ref, sems,
):
    copies = Copies(sems)
    times = place_temporal(place_ref, mine_ref, other_ref, time_ref, copies)
    loads = spatial_loads(0, full_ref, contrasted_ref, strip_ref, held_ref, copies)
    for load in times:
        load.wait()
    gram_ref[...] = (nt(time_ref[...], time_ref[...]) * (1.0 / math.sqrt(time_ref.shape[0]))).astype(BF16)
    spatial_half(
        0, place_ref, time_ref, gram_ref, send_ref, keep_ref, rows_ref, weight_ref, strip_ref, held_ref, loads
    )


def per_device(
    movie, offsets, spatial, temporal, step_spatial, step_temporal, thresh_spatial, thresh_temporal
):
    slab, strip = spatial.shape
    shard, span = temporal.shape
    rank = slab * lax.axis_size("tm")
    pixels = strip * lax.axis_size("pix")
    frames = span * lax.axis_size("tm")
    pix = lax.axis_index("pix")
    tm = lax.axis_index("tm")
    x, yhi, core = pix >> 2, (pix >> 1) & 1, pix & 1
    place = jnp.stack([tm, x, core]).astype(jnp.int32)

    def own(a, index, rows):
        return lax.dynamic_slice_in_dim(a, index * rows, rows, 0)[:, None]

    def own_temporal(a):
        across = x ^ (3 - 2 * core)
        return jnp.concatenate([own(a, at * 4 + y * 2 + core, shard) for at in (x, across) for y in range(2)])

    def own_spatial(a, mask):
        return jnp.concatenate([own(a, tm, slab), own(a, tm ^ mask, slab)])

    coef_temporal = own_temporal(step_temporal * (math.sqrt(rank) / pixels))
    limit_temporal = own_temporal(thresh_temporal)
    all_spatial = step_spatial * (math.sqrt(rank) / frames)
    coef_spatial = [own_spatial(all_spatial, order[2]) for _, _, order in PARTS]
    limit_spatial = [own_spatial(thresh_spatial, order[2]) for _, _, order in PARTS]

    def second_gather(slabs):
        return [jnp.concatenate([s, hop(s, "tm", order[1])]) for s, (_, _, order) in zip(slabs, PARTS)]

    def first_gather(near):
        return [(a, hop(a, "tm", order[0])) for a, (_, _, order) in zip(near, PARTS)]

    def gather_temporal(quad):
        mine = jnp.concatenate([quad, hop_x(quad, 0)])
        return mine, hop(mine, "pix", 1)

    shards = [spatial[:, begin : begin + width] for begin, width, _ in PARTS]
    size = lax.axis_size("pix")
    up = [(i, i + 1) for i in range(size - 1)]
    down = [(j, i) for i, j in up]
    before = lax.ppermute(movie[movie.shape[0] - EDGE :], "pix", up)
    after = lax.ppermute(movie[:EDGE], "pix", down)
    slabs = [jnp.concatenate([s, hop(s, "tm", order[2])]) for s, (_, _, order) in zip(shards, PARTS)]
    across = hop(temporal, "pix", 2)
    pair = jnp.concatenate([jnp.where(yhi == 0, temporal, across), jnp.where(yhi == 0, across, temporal)])
    near = second_gather(slabs)
    near, before, after = lax.optimization_barrier((near, before, after))
    pieces = first_gather(near)
    quad = jnp.concatenate([pair, hop_x(pair, 1)])
    contrasted = contrast(movie, before, after, offsets, near[1])
    mine, other = gather_temporal(quad)

    half = rank // 2
    for turn in range(ROUNDS):
        scratch = [
            pltpu.VMEM((half, strip), BF16),
            pltpu.VMEM((half, rank), BF16),
            pltpu.VMEM((strip, span), BF16),
            COPIES,
        ]
        full, time, stored, send = pl.pallas_call(
            temporal_send,
            out_shape=[
                jax.ShapeDtypeStruct((rank, strip), BF16),
                jax.ShapeDtypeStruct((rank, span), BF16),
                pltpu.HBM((rank, strip), BF16),
                jax.ShapeDtypeStruct((half, span), BF16),
            ],
            in_specs=[SMEM] + [ANY] * 6 + [HBM, ANY, ANY],
            out_specs=[VMEM, VMEM, HBM, VMEM],
            scratch_shapes=scratch,
            compiler_params=PARAMS,
        )(place, *[piece for both in pieces for piece in both], in_hbm(contrasted), mine, other)
        got = hop(send, "pix", 1)
        keep = pl.pallas_call(
            temporal_keep,
            out_shape=jax.ShapeDtypeStruct((half, span), F32),
            in_specs=[SMEM, VMEM, HBM, VMEM],
            out_specs=VMEM,
            scratch_shapes=scratch,
            compiler_params=PARAMS,
        )(place, full, in_hbm(contrasted), time)
        grad = keep + got.astype(F32)
        grad = grad[: half // 2] + hop_x(grad[half // 2 :].astype(BF16), 0).astype(F32)
        mine_sum = grad.astype(BF16)
        got = hop_x(mine_sum, 1)
        swapped = jnp.concatenate([got[half // 4 :], got[: half // 4]])
        mine_sum = (mine_sum.astype(F32) + swapped.astype(F32)).astype(BF16)
        grad = mine_sum.astype(F32) + hop(mine_sum, "pix", 2).astype(F32)
        quad = soften(quad.astype(F32) + coef_temporal * grad, limit_temporal).astype(BF16)
        mine, other = gather_temporal(quad)

        def part_shapes(part):
            width = PARTS[part][1]
            return [jax.ShapeDtypeStruct((half, width), BF16), jax.ShapeDtypeStruct((half, width), F32)]

        widest = max(width for _, width, _ in PARTS)
        scratch = [
            pltpu.VMEM((rank, span), BF16),
            pltpu.VMEM((rank, rank), BF16),
            pltpu.VMEM((rank, widest), BF16),
            pltpu.VMEM((widest, span), BF16),
            COPIES,
        ]
        send, keep, time, gram = pl.pallas_call(
            spatial_first,
            out_shape=part_shapes(0)
            + [jax.ShapeDtypeStruct((rank, span), BF16), jax.ShapeDtypeStruct((rank, rank), BF16)],
            in_specs=[SMEM, HBM, HBM, ANY, ANY],
            out_specs=[VMEM] * 4,
            scratch_shapes=scratch,
            compiler_params=PARAMS,
        )(place, in_hbm(stored), in_hbm(contrasted), mine, other)
        grads = [(send, keep)]
        for part in (1, 2):
            grads.append(
                pl.pallas_call(
                    functools.partial(spatial_part, part),
                    out_shape=part_shapes(part),
                    in_specs=[SMEM, HBM, HBM, VMEM, VMEM],
                    out_specs=[VMEM] * 2,
                    scratch_shapes=scratch,
                    compiler_params=PARAMS,
                )(place, in_hbm(stored), in_hbm(contrasted), time, gram)
            )
        totals = [
            keep + hop(send, "tm", order[0]).astype(F32) for (send, keep), (_, _, order) in zip(grads, PARTS)
        ]
        totals = [
            total[: 2 * slab] + hop(total[2 * slab :].astype(BF16), "tm", order[1]).astype(F32)
            for total, (_, _, order) in zip(totals, PARTS)
        ]
        if turn < ROUNDS - 1:
            sums = []
            for total, (_, _, order) in zip(totals, PARTS):
                mine_sum = total.astype(BF16)
                got = hop(mine_sum, "tm", order[2])
                swapped = jnp.concatenate([got[slab:], got[:slab]])
                sums.append(mine_sum.astype(F32) + swapped.astype(F32))
            slabs = [
                soften(s.astype(F32) + coef * g, limit).astype(BF16)
                for s, g, coef, limit in zip(slabs, sums, coef_spatial, limit_spatial)
            ]
            pieces = first_gather(second_gather(slabs))
        else:
            sums = [
                total[:slab] + hop(total[slab:].astype(BF16), "tm", order[2]).astype(F32)
                for total, (_, _, order) in zip(totals, PARTS)
            ]
            shards = [
                soften(s[:slab].astype(F32) + coef[:slab] * g, limit[:slab]).astype(BF16)
                for s, g, coef, limit in zip(slabs, sums, coef_spatial, limit_spatial)
            ]
    temporal_out = jnp.where(yhi == 0, quad[:shard], quad[shard : 2 * shard])
    return jnp.concatenate(shards, 1), temporal_out


def solution(mesh):
    placed = (P("pix", "tm"), P(), P("tm", "pix"), P("pix", "tm"), P(), P(), P(), P())
    return jax.shard_map(
        per_device,
        mesh=mesh,
        in_specs=placed,
        out_specs=(P("tm", "pix"), P("pix", "tm")),
        check_vma=False,
    )
```

time: 236 us -> 241 us (1.021)
  Pallas kernels: 25.9 us -> 59.7 us
  local copies, waits for them, and re-layouts: 20.2 us -> 5.17 us
  waiting for transfers between devices: 81 us -> 95 us
  blocking collectives: 13.3 us -> 0 us
  starting transfers between devices: 78.8 us -> 69.2 us
  other arithmetic: 10.8 us -> 5.62 us
    pallas_call x5 -> x11, Pallas kernels: 25.9 us -> 59.7 us  [the longest x4 16.3 us: per_device(): pl.pallas_call(functools.partial(spatial_part, part), out_shape=part_shap...]
    ppermute x11 -> x10, waiting for transfers between devices: 13.5 us -> 35 us  [the longest x8 35 us: hop_x(): lax.ppermute(a, 'pix', [(i, i ^ 4 * (1 if i % 2 == second else 3)) for i...]
    unnamed x84 -> x46, local copies, waits for them, and re-layouts: 16 us -> 1.77 us
    all_to_all x1 -> x0, blocking collectives: 13.3 us -> none  [per_device(): lax.all_to_all(grad.reshape(4, 2 * temporal_rows, span), 'pix', 0, 0, axi...]
    ppermute x41, starting transfers between devices: 57.3 us -> 46.9 us  [hop(): return lax.ppermute(a, axis, [(i, i ^ mask) for i in range(size)])]
    all_to_all x1 -> x0, waiting for transfers between devices: 9.62 us -> none  [per_device(): lax.all_to_all(grad.reshape(4, 2 * temporal_rows, span), 'pix', 0, 0, axi...]
    ppermute x11 -> x10, starting transfers between devices: 16.9 us -> 22.3 us  [the longest x8 19.7 us: hop_x(): lax.ppermute(a, 'pix', [(i, i ^ 4 * (1 if i % 2 == second else 3)) for i...]
    all_to_all x1 -> x0, starting transfers between devices: 4.54 us -> none  [per_device(): lax.all_to_all(grad.reshape(4, 2 * temporal_rows, span), 'pix', 0, 0, axi...]
  transfers between devices with their start and end apart: 53 -> 51, of which waited for: 32 -> 28; matrix products, arithmetic and copies ran while one was open for 4% -> 3% of each run, Pallas kernels for 2% -> 12%
where the time goes in v3:
time: 241 us; the launch traced here: 236 us
  waiting for transfers between devices  95 us (39%)
  starting transfers between devices  69.2 us (29%)
  Pallas kernels  59.7 us (25%)
  other arithmetic  5.62 us (2%)
  local copies, waits for them, and re-layouts  5.17 us (2%)
    ppermute x41, waiting for transfers between devices, hop(): return lax.ppermute(a, axis, [(i, i ^ mask) for i in range(size)])  60.1 us
    ppermute x41, starting transfers between devices, hop(): return lax.ppermute(a, axis, [(i, i ^ mask) for i in range(size)])  46.9 us
    ppermute x8, waiting for transfers between devices, hop_x(): lax.ppermute(a, 'pix', [(i, i ^ 4 * (1 if i % 2 == second else 3)) for i...  35 us
    ppermute x8, starting transfers between devices, hop_x(): lax.ppermute(a, 'pix', [(i, i ^ 4 * (1 if i % 2 == second else 3)) for i...  19.7 us
    pallas_call x4, Pallas kernels, per_device(): pl.pallas_call(functools.partial(spatial_part, part), out_shape=part_shap...  16.3 us
    pallas_call x2, Pallas kernels, per_device(): pl.pallas_call(temporal_send, out_shape=[jax.ShapeDtypeStruct((rank, stri...  12.9 us
    pallas_call x2, Pallas kernels, per_device(): pl.pallas_call(temporal_keep, out_shape=jax.ShapeDtypeStruct((half, span)...  11.5 us
    pallas_call x2, Pallas kernels, per_device(): pl.pallas_call(spatial_first, out_shape=part_shapes(0) + [jax.ShapeDtypeS...  10.8 us
  transfers between devices with their start and end apart: 51, of which 28 were waited for; matrix products, arithmetic and copies ran while one was open for 3% of the time, Pallas kernels for 12%

profile of v3, /device:TPU:0, one launch (start us, length us, event | category | flops | bytes accessed | tf_op | source)
XLA Modules:
  0.0 236.4 jit_solution(9962636538757683345)
XLA Ops:
  19.5 5.7 %collective-permute-start.13 = (bf16[128,1024]{1,0:T(8,128)(2,1)S(1)}, bf16[128,1024]{1,0:T(8,128)(2,1)S(1)}, u32[]{:S(2)}, u32[]{:S(2)}) collective-permute-start(bf16[128,1024]{1,0:T(8,128)(2,1)S(1)} %pad_maximum_fusion.9), channel_id=1, source_target_pairs={{0,32},{8,104},{16,48},{24,120},{32,0},{40,72},{48,16},{56,88},{64... | collective-permute-start | bytes 786440 | tf_op jit(solution)/shard_map/ppermute | solution.py:35
  27.1 4.6 %collective-permute-done.13 = bf16[128,1024]{1,0:T(8,128)(2,1)S(1)} collective-permute-done((bf16[128,1024]{1,0:T(8,128)(2,1)S(1)}, bf16[128,1024]{1,0:T(8,128)(2,1)S(1)}, u32[]{:S(2)}, u32[]{:S(2)}) %collective-permute-start.13) | collective-permute-done | bytes 262176 | tf_op jit(solution)/shard_map/ppermute | solution.py:35
  38.1 8.2 %shard_map.95.contrasted_ref = bf16[2048,1024]{1,0:T(8,128)(2,1)} custom-call(s32[8]{0:T(128)S(1)} %copy-done.2, bf16[2048,1024]{1,0:T(8,128)(2,1)} %movie_ref.1, bf16[144,1024]{1,0:T(8,128)(2,1)S(1)} %collective-permute-done.6.before_ref, bf16[144,1024]{1,0:T(8,128)(2,1)S(1)} %copy-done.1, bf16[256,768]{1,0:T(8,128)(2,1)S(1)} %pad_maximum_fusion.3.later_ref.a1), custom_call_target="tpu_custom_call" | custom-call | tf_op jit(solution)/shard_map/pallas_call | solution.py:110
  46.3 6.5 %shard_map.96 = (bf16[512,2048]{1,0:T(8,128)(2,1)S(1)}, bf16[512,1024]{1,0:T(8,128)(2,1)S(1)}, bf16[512,2048]{1,0:T(8,128)(2,1)}, bf16[256,1024]{1,0:T(8,128)(2,1)S(1)}) custom-call(s32[3]{0:T(128)S(1)} %pad_add_fusion.place_ref, bf16[256,640]{1,0:T(8,128)(2,1)S(1)} %pad_maximum_fusion.5.a0, bf16[256,640]{1,0:T(8,128)(2,1)S(1)} %collective-permute-done.8.b0, ...), custom_call_target="tpu_custom_call" | custom-call | tf_op jit(solution)/shard_map/pallas_call | solution.py:327
  52.9 5.7 %shard_map.97 = f32[256,1024]{1,0:T(8,128)S(1)} custom-call(s32[3]{0:T(128)S(1)} %pad_add_fusion.place_ref, bf16[512,2048]{1,0:T(8,128)(2,1)S(1)} %get-tuple-element.37.full_ref, bf16[2048,1024]{1,0:T(8,128)(2,1)} %shard_map.95.contrasted_ref, bf16[512,1024]{1,0:T(8,128)(2,1)S(1)} %get-tuple-element.38.time_ref), custom_call_target="tpu_custom_call" | custom-call | tf_op jit(solution)/shard_map/pallas_call | solution.py:341
  61.5 4.3 %collective-permute-done.16 = bf16[128,1024]{1,0:T(8,128)(2,1)S(1)} collective-permute-done((bf16[128,1024]{1,0:T(8,128)(2,1)S(1)}, bf16[128,1024]{1,0:T(8,128)(2,1)S(1)}, u32[]{:S(2)}, u32[]{:S(2)}) %collective-permute-start.16) | collective-permute-done | bytes 262176 | tf_op jit(solution)/shard_map/ppermute | solution.py:35
  68.3 5.2 %collective-permute-done.17 = bf16[128,1024]{1,0:T(8,128)(2,1)S(1)} collective-permute-done((bf16[128,1024]{1,0:T(8,128)(2,1)S(1)}, bf16[128,1024]{1,0:T(8,128)(2,1)S(1)}, u32[]{:S(2)}, u32[]{:S(2)}) %collective-permute-start.17) | collective-permute-done | bytes 262176 | tf_op jit(solution)/shard_map/ppermute | solution.py:35
  77.1 4.7 %collective-permute-done.18 = bf16[128,1024]{1,0:T(8,128)(2,1)S(1)} collective-permute-done((bf16[128,1024]{1,0:T(8,128)(2,1)S(1)}, bf16[128,1024]{1,0:T(8,128)(2,1)S(1)}, u32[]{:S(2)}, u32[]{:S(2)}) %collective-permute-start.18) | collective-permute-done | bytes 262176 | tf_op jit(solution)/shard_map/ppermute | solution.py:30
  83.6 5.0 %collective-permute-done.19 = bf16[128,1024]{1,0:T(8,128)(2,1)S(1)} collective-permute-done((bf16[128,1024]{1,0:T(8,128)(2,1)S(1)}, bf16[128,1024]{1,0:T(8,128)(2,1)S(1)}, u32[]{:S(2)}, u32[]{:S(2)}) %collective-permute-start.19) | collective-permute-done | bytes 262176 | tf_op jit(solution)/shard_map/ppermute | solution.py:35
  90.6 5.4 %shard_map.98 = (bf16[256,640]{1,0:T(8,128)(2,1)S(1)}, f32[256,640]{1,0:T(8,128)S(1)}, bf16[512,1024]{1,0:T(8,128)(2,1)S(1)}, bf16[512,512]{1,0:T(8,128)(2,1)S(1)}) custom-call(s32[3]{0:T(128)S(1)} %pad_add_fusion.place_ref, bf16[512,2048]{1,0:T(8,128)(2,1)} %get-tuple-element.36.full_ref, bf16[2048,1024]{1,0:T(8,128)(2,1)} %shard_map.95.contrasted_ref, ...), custom_call_target="tpu_custom_call" | custom-call | tf_op jit(solution)/shard_map/pallas_call | solution.py:371
  96.1 4.0 %shard_map.100 = (bf16[256,640]{1,0:T(8,128)(2,1)S(1)}, f32[256,640]{1,0:T(8,128)S(1)}) custom-call(s32[3]{0:T(128)S(1)} %pad_add_fusion.place_ref, bf16[512,2048]{1,0:T(8,128)(2,1)} %get-tuple-element.36.full_ref, bf16[2048,1024]{1,0:T(8,128)(2,1)} %shard_map.95.contrasted_ref, bf16[512,1024]{1,0:T(8,128)(2,1)S(1)} %get-tuple-element.42.time_ref, ...), custom_call_target="tpu_custom_call" | custom-call | tf_op jit(solution)/shard_map/pallas_call | solution.py:383
  104.6 4.1 %shard_map.99 = (bf16[256,768]{1,0:T(8,128)(2,1)S(1)}, f32[256,768]{1,0:T(8,128)S(1)}) custom-call(s32[3]{0:T(128)S(1)} %pad_add_fusion.place_ref, bf16[512,2048]{1,0:T(8,128)(2,1)} %get-tuple-element.36.full_ref, bf16[2048,1024]{1,0:T(8,128)(2,1)} %shard_map.95.contrasted_ref, bf16[512,1024]{1,0:T(8,128)(2,1)S(1)} %get-tuple-element.42.time_ref, ...), custom_call_target="tpu_custom_call" | custom-call | tf_op jit(solution)/shard_map/pallas_call | solution.py:383
  114.0 6.8 %collective-permute-done.26 = bf16[256,768]{1,0:T(8,128)(2,1)S(1)} collective-permute-done((bf16[256,768]{1,0:T(8,128)(2,1)S(1)}, bf16[256,768]{1,0:T(8,128)(2,1)S(1)}, u32[]{:S(2)}, u32[]{:S(2)}) %collective-permute-start.26) | collective-permute-done | bytes 393248 | tf_op jit(solution)/shard_map/ppermute | solution.py:30
  144.7 6.9 %collective-permute-done.25.b0 = bf16[256,640]{1,0:T(8,128)(2,1)S(1)} collective-permute-done((bf16[256,640]{1,0:T(8,128)(2,1)S(1)}, bf16[256,640]{1,0:T(8,128)(2,1)S(1)}, u32[]{:S(2)}, u32[]{:S(2)}) %collective-permute-start.25) | collective-permute-done | bytes 327712 | tf_op jit(solution)/shard_map/ppermute | solution.py:30
  151.6 6.5 %shard_map.101 = (bf16[512,2048]{1,0:T(8,128)(2,1)S(1)}, bf16[512,1024]{1,0:T(8,128)(2,1)S(1)}, bf16[512,2048]{1,0:T(8,128)(2,1)}, bf16[256,1024]{1,0:T(8,128)(2,1)S(1)}) custom-call(s32[3]{0:T(128)S(1)} %pad_add_fusion.place_ref, bf16[256,640]{1,0:T(8,128)(2,1)S(1)} %pad_maximum_fusion.7.a0, bf16[256,640]{1,0:T(8,128)(2,1)S(1)} %collective-permute-done.25.b0, ...), custom_call_target="tpu_custom_call" | custom-call | tf_op jit(solution)/shard_map/pallas_call | solution.py:327
  158.1 5.7 %shard_map.102 = f32[256,1024]{1,0:T(8,128)S(1)} custom-call(s32[3]{0:T(128)S(1)} %pad_add_fusion.place_ref, bf16[512,2048]{1,0:T(8,128)(2,1)S(1)} %get-tuple-element.49.full_ref, bf16[2048,1024]{1,0:T(8,128)(2,1)} %shard_map.95.contrasted_ref, bf16[512,1024]{1,0:T(8,128)(2,1)S(1)} %get-tuple-element.50.time_ref), custom_call_target="tpu_custom_call" | custom-call | tf_op jit(solution)/shard_map/pallas_call | solution.py:341
  165.6 4.9 %collective-permute-done.37 = bf16[128,1024]{1,0:T(8,128)(2,1)S(1)} collective-permute-done((bf16[128,1024]{1,0:T(8,128)(2,1)S(1)}, bf16[128,1024]{1,0:T(8,128)(2,1)S(1)}, u32[]{:S(2)}, u32[]{:S(2)}) %collective-permute-start.37) | collective-permute-done | bytes 262176 | tf_op jit(solution)/shard_map/ppermute | solution.py:35
  173.3 5.0 %collective-permute-done.38 = bf16[128,1024]{1,0:T(8,128)(2,1)S(1)} collective-permute-done((bf16[128,1024]{1,0:T(8,128)(2,1)S(1)}, bf16[128,1024]{1,0:T(8,128)(2,1)S(1)}, u32[]{:S(2)}, u32[]{:S(2)}) %collective-permute-start.38) | collective-permute-done | bytes 262176 | tf_op jit(solution)/shard_map/ppermute | solution.py:35
  181.2 5.5 %collective-permute-done.39 = bf16[128,1024]{1,0:T(8,128)(2,1)S(1)} collective-permute-done((bf16[128,1024]{1,0:T(8,128)(2,1)S(1)}, bf16[128,1024]{1,0:T(8,128)(2,1)S(1)}, u32[]{:S(2)}, u32[]{:S(2)}) %collective-permute-start.39) | collective-permute-done | bytes 262176 | tf_op jit(solution)/shard_map/ppermute | solution.py:30
  187.5 5.9 %collective-permute-done.40 = bf16[128,1024]{1,0:T(8,128)(2,1)S(1)} collective-permute-done((bf16[128,1024]{1,0:T(8,128)(2,1)S(1)}, bf16[128,1024]{1,0:T(8,128)(2,1)S(1)}, u32[]{:S(2)}, u32[]{:S(2)}) %collective-permute-start.40) | collective-permute-done | bytes 262176 | tf_op jit(solution)/shard_map/ppermute | solution.py:35
  195.4 5.4 %shard_map.103 = (bf16[256,640]{1,0:T(8,128)(2,1)S(1)}, f32[256,640]{1,0:T(8,128)S(1)}, bf16[512,1024]{1,0:T(8,128)(2,1)S(1)}, bf16[512,512]{1,0:T(8,128)(2,1)S(1)}) custom-call(s32[3]{0:T(128)S(1)} %pad_add_fusion.place_ref, bf16[512,2048]{1,0:T(8,128)(2,1)} %get-tuple-element.48.full_ref, bf16[2048,1024]{1,0:T(8,128)(2,1)} %shard_map.95.contrasted_ref, ...), custom_call_target="tpu_custom_call" | custom-call | tf_op jit(solution)/shard_map/pallas_call | solution.py:371
  200.8 4.0 %shard_map.105 = (bf16[256,640]{1,0:T(8,128)(2,1)S(1)}, f32[256,640]{1,0:T(8,128)S(1)}) custom-call(s32[3]{0:T(128)S(1)} %pad_add_fusion.place_ref, bf16[512,2048]{1,0:T(8,128)(2,1)} %get-tuple-element.48.full_ref, bf16[2048,1024]{1,0:T(8,128)(2,1)} %shard_map.95.contrasted_ref, bf16[512,1024]{1,0:T(8,128)(2,1)S(1)} %get-tuple-element.54.time_ref, ...), custom_call_target="tpu_custom_call" | custom-call | tf_op jit(solution)/shard_map/pallas_call | solution.py:383
  206.4 4.1 %shard_map.104 = (bf16[256,768]{1,0:T(8,128)(2,1)S(1)}, f32[256,768]{1,0:T(8,128)S(1)}) custom-call(s32[3]{0:T(128)S(1)} %pad_add_fusion.place_ref, bf16[512,2048]{1,0:T(8,128)(2,1)} %get-tuple-element.48.full_ref, bf16[2048,1024]{1,0:T(8,128)(2,1)} %shard_map.95.contrasted_ref, bf16[512,1024]{1,0:T(8,128)(2,1)S(1)} %get-tuple-element.54.time_ref, ...), custom_call_target="tpu_custom_call" | custom-call | tf_op jit(solution)/shard_map/pallas_call | solution.py:383
  216.9 5.8 %collective-permute-done.45 = bf16[256,768]{1,0:T(8,128)(2,1)S(1)} collective-permute-done((bf16[256,768]{1,0:T(8,128)(2,1)S(1)}, bf16[256,768]{1,0:T(8,128)(2,1)S(1)}, u32[]{:S(2)}, u32[]{:S(2)}) %collective-permute-start.45) | collective-permute-done | bytes 393248 | tf_op jit(solution)/shard_map/ppermute | solution.py:30
  (207 shorter events, 104.7 us)
Async XLA Ops:
  0.6 10.5 %collective-permute-start.11 = (bf16[32,1024]{1,0:T(8,128)(2,1)}, bf16[32,1024]{1,0:T(8,128)(2,1)S(1)}, u32[]{:S(2)}, u32[]{:S(2)}) collective-permute-start(bf16[32,1024]{1,0:T(8,128)(2,1)} %param.11), channel_id=1, source_target_pairs={{0,16},{8,24},{16,0},{24,8},{32,48},{40,56},{48,32},{56,40},{64,80... | collective-permute-start | bytes 196616 | tf_op jit(solution)/shard_map/ppermute | solution.py:30
  5.0 12.3 %collective-permute-start.4 = (bf16[64,640]{1,0:T(8,128)(2,1)S(1)}, bf16[64,640]{1,0:T(8,128)(2,1)S(1)}, u32[]{:S(2)}, u32[]{:S(2)}) collective-permute-start(bf16[64,640]{1,0:T(8,128)(2,1)S(1)} %get-tuple-element.68), channel_id=1, source_target_pairs={{0,4},{1,5},{2,6},{3,7},{4,0},{5,1},{6,2},{7,3},{8,12},{9,13},{10,... | collective-permute-start | bytes 245768 | tf_op jit(solution)/shard_map/ppermute | solution.py:30
  5.7 13.8 %collective-permute-start = (bf16[64,640]{1,0:T(8,128)(2,1)S(1)}, bf16[64,640]{1,0:T(8,128)(2,1)S(1)}, u32[]{:S(2)}, u32[]{:S(2)}) collective-permute-start(bf16[64,640]{1,0:T(8,128)(2,1)S(1)} %get-tuple-element.69), channel_id=1, source_target_pairs={{0,1},{1,0},{2,3},{3,2},{4,5},{5,4},{6,7},{7,6},{8,9},{9,8},{10,11... | collective-permute-start | bytes 245768 | tf_op jit(solution)/shard_map/ppermute | solution.py:30
  8.5 16.6 %collective-permute-start.2 = (bf16[64,768]{1,0:T(8,128)(2,1)S(1)}, bf16[64,768]{1,0:T(8,128)(2,1)S(1)}, u32[]{:S(2)}, u32[]{:S(2)}) collective-permute-start(bf16[64,768]{1,0:T(8,128)(2,1)S(1)} %slice.138), channel_id=1, source_target_pairs={{0,3},{1,2},{2,1},{3,0},{4,7},{5,6},{6,5},{7,4},{8,11},{9,10},{10,... | collective-permute-start | bytes 294920 | tf_op jit(solution)/shard_map/ppermute | solution.py:30
  16.0 18.2 %collective-permute-start.6 = (bf16[144,1024]{1,0:T(8,128)(2,1)S(1)}, bf16[144,1024]{1,0:T(8,128)(2,1)S(1)}, u32[]{:S(2)}, u32[]{:S(2)}) collective-permute-start(bf16[144,1024]{1,0:T(8,128)(2,1)S(1)} %get-tuple-element.63), channel_id=1, source_target_pairs={{0,8},{8,16},{16,24},{24,32},{32,40},{40,48},{48,56},{56,64},{64,7... | collective-permute-start | bytes 884744 | tf_op jit(solution)/shard_map/ppermute | solution.py:307
  17.3 16.9 %collective-permute-start.7 = (bf16[144,1024]{1,0:T(8,128)(2,1)S(1)}, bf16[144,1024]{1,0:T(8,128)(2,1)S(1)}, u32[]{:S(2)}, u32[]{:S(2)}) collective-permute-start(bf16[144,1024]{1,0:T(8,128)(2,1)S(1)} %get-tuple-element.62), channel_id=1, source_target_pairs={{8,0},{16,8},{24,16},{32,24},{40,32},{48,40},{56,48},{64,56},{72,6... | collective-permute-start | bytes 884744 | tf_op jit(solution)/shard_map/ppermute | solution.py:308
  19.5 12.2 %collective-permute-start.13 = (bf16[128,1024]{1,0:T(8,128)(2,1)S(1)}, bf16[128,1024]{1,0:T(8,128)(2,1)S(1)}, u32[]{:S(2)}, u32[]{:S(2)}) collective-permute-start(bf16[128,1024]{1,0:T(8,128)(2,1)S(1)} %pad_maximum_fusion.9), channel_id=1, source_target_pairs={{0,32},{8,104},{16,48},{24,120},{32,0},{40,72},{48,16},{56,88},{64... | collective-permute-start | bytes 786440 | tf_op jit(solution)/shard_map/ppermute | solution.py:35
  31.8 14.6 %collective-permute-start.14 = (bf16[256,1024]{1,0:T(8,128)(2,1)S(1)}, bf16[256,1024]{1,0:T(8,128)(2,1)S(1)}, u32[]{:S(2)}, u32[]{:S(2)}) collective-permute-start(bf16[256,1024]{1,0:T(8,128)(2,1)S(1)} %pad_maximum_fusion.mine_ref), channel_id=1, source_target_pairs={{0,8},{8,0},{16,24},{24,16},{32,40},{40,32},{48,56},{56,48},{64,72... | collective-permute-start | bytes 1572872 | tf_op jit(solution)/shard_map/ppermute | solution.py:30
  34.9 11.4 %collective-permute-start.9 = (bf16[256,768]{1,0:T(8,128)(2,1)S(1)}, bf16[256,768]{1,0:T(8,128)(2,1)S(1)}, u32[]{:S(2)}, u32[]{:S(2)}) collective-permute-start(bf16[256,768]{1,0:T(8,128)(2,1)S(1)} %pad_maximum_fusion.3.later_ref.a1), channel_id=1, source_target_pairs={{0,4},{1,5},{2,6},{3,7},{4,0},{5,1},{6,2},{7,3},{8,12},{9,13},{10,... | collective-permute-start | bytes 1179656 | tf_op jit(solution)/shard_map/ppermute | solution.py:30
  35.8 10.5 %collective-permute-start.10 = (bf16[256,640]{1,0:T(8,128)(2,1)S(1)}, bf16[256,640]{1,0:T(8,128)(2,1)S(1)}, u32[]{:S(2)}, u32[]{:S(2)}) collective-permute-start(bf16[256,640]{1,0:T(8,128)(2,1)S(1)} %pad_maximum_fusion.6.a2), channel_id=1, source_target_pairs={{0,1},{1,0},{2,3},{3,2},{4,5},{5,4},{6,7},{7,6},{8,9},{9,8},{10,11... | collective-permute-start | bytes 983048 | tf_op jit(solution)/shard_map/ppermute | solution.py:30
  36.1 10.2 %collective-permute-start.8 = (bf16[256,640]{1,0:T(8,128)(2,1)S(1)}, bf16[256,640]{1,0:T(8,128)(2,1)S(1)}, u32[]{:S(2)}, u32[]{:S(2)}) collective-permute-start(bf16[256,640]{1,0:T(8,128)(2,1)S(1)} %pad_maximum_fusion.5.a0), channel_id=1, source_target_pairs={{0,3},{1,2},{2,1},{3,0},{4,7},{5,6},{6,5},{7,4},{8,11},{9,10},{10,... | collective-permute-start | bytes 983048 | tf_op jit(solution)/shard_map/ppermute | solution.py:30
  100.1 9.8 %collective-permute-start.31 = (bf16[256,640]{1,0:T(8,128)(2,1)S(1)}, bf16[256,640]{1,0:T(8,128)(2,1)S(1)}, u32[]{:S(2)}, u32[]{:S(2)}) collective-permute-start(bf16[256,640]{1,0:T(8,128)(2,1)S(1)} %get-tuple-element.47), channel_id=1, source_target_pairs={{0,1},{1,0},{2,3},{3,2},{4,5},{5,4},{6,7},{7,6},{8,9},{9,8},{10,11... | collective-permute-start | bytes 983048 | tf_op jit(solution)/shard_map/ppermute | solution.py:30
  101.9 11.0 %collective-permute-start.21 = (bf16[256,640]{1,0:T(8,128)(2,1)S(1)}, bf16[256,640]{1,0:T(8,128)(2,1)S(1)}, u32[]{:S(2)}, u32[]{:S(2)}) collective-permute-start(bf16[256,640]{1,0:T(8,128)(2,1)S(1)} %get-tuple-element.41), channel_id=1, source_target_pairs={{0,3},{1,2},{2,1},{3,0},{4,7},{5,6},{6,5},{7,4},{8,11},{9,10},{10,... | collective-permute-start | bytes 983048 | tf_op jit(solution)/shard_map/ppermute | solution.py:30
  108.7 12.1 %collective-permute-start.26 = (bf16[256,768]{1,0:T(8,128)(2,1)S(1)}, bf16[256,768]{1,0:T(8,128)(2,1)S(1)}, u32[]{:S(2)}, u32[]{:S(2)}) collective-permute-start(bf16[256,768]{1,0:T(8,128)(2,1)S(1)} %get-tuple-element.45), channel_id=1, source_target_pairs={{0,4},{1,5},{2,6},{3,7},{4,0},{5,1},{6,2},{7,3},{8,12},{9,13},{10,... | collective-permute-start | bytes 1179656 | tf_op jit(solution)/shard_map/ppermute | solution.py:30
  110.0 11.1 %collective-permute-start.32 = (bf16[128,640]{1,0:T(8,128)(2,1)S(1)}, bf16[128,640]{1,0:T(8,128)(2,1)S(1)}, u32[]{:S(2)}, u32[]{:S(2)}) collective-permute-start(bf16[128,640]{1,0:T(8,128)(2,1)S(1)} %slice.277), channel_id=1, source_target_pairs={{0,3},{1,2},{2,1},{3,0},{4,7},{5,6},{6,5},{7,4},{8,11},{9,10},{10,... | collective-permute-start | bytes 491528 | tf_op jit(solution)/shard_map/ppermute | solution.py:30
  112.9 11.4 %collective-permute-start.22 = (bf16[128,640]{1,0:T(8,128)(2,1)S(1)}, bf16[128,640]{1,0:T(8,128)(2,1)S(1)}, u32[]{:S(2)}, u32[]{:S(2)}) collective-permute-start(bf16[128,640]{1,0:T(8,128)(2,1)S(1)} %slice.278), channel_id=1, source_target_pairs={{0,4},{1,5},{2,6},{3,7},{4,0},{5,1},{6,2},{7,3},{8,12},{9,13},{10,... | collective-permute-start | bytes 491528 | tf_op jit(solution)/shard_map/ppermute | solution.py:30
  141.2 10.4 %collective-permute-start.30 = (bf16[256,768]{1,0:T(8,128)(2,1)S(1)}, bf16[256,768]{1,0:T(8,128)(2,1)S(1)}, u32[]{:S(2)}, u32[]{:S(2)}) collective-permute-start(bf16[256,768]{1,0:T(8,128)(2,1)S(1)} %pad_maximum_fusion.4.a1), channel_id=1, source_target_pairs={{0,4},{1,5},{2,6},{3,7},{4,0},{5,1},{6,2},{7,3},{8,12},{9,13},{10,... | collective-permute-start | bytes 1179656 | tf_op jit(solution)/shard_map/ppermute | solution.py:30
  142.8 8.8 %collective-permute-start.25 = (bf16[256,640]{1,0:T(8,128)(2,1)S(1)}, bf16[256,640]{1,0:T(8,128)(2,1)S(1)}, u32[]{:S(2)}, u32[]{:S(2)}) collective-permute-start(bf16[256,640]{1,0:T(8,128)(2,1)S(1)} %pad_maximum_fusion.7.a0), channel_id=1, source_target_pairs={{0,3},{1,2},{2,1},{3,0},{4,7},{5,6},{6,5},{7,4},{8,11},{9,10},{10,... | collective-permute-start | bytes 983048 | tf_op jit(solution)/shard_map/ppermute | solution.py:30
  178.3 8.3 %collective-permute-start.39 = (bf16[128,1024]{1,0:T(8,128)(2,1)S(1)}, bf16[128,1024]{1,0:T(8,128)(2,1)S(1)}, u32[]{:S(2)}, u32[]{:S(2)}) collective-permute-start(bf16[128,1024]{1,0:T(8,128)(2,1)S(1)} %add_convert_fusion), channel_id=1, source_target_pairs={{0,16},{8,24},{16,0},{24,8},{32,48},{40,56},{48,32},{56,40},{64,80... | collective-permute-start | bytes 786440 | tf_op jit(solution)/shard_map/ppermute | solution.py:30
  204.8 9.8 %collective-permute-start.48 = (bf16[256,640]{1,0:T(8,128)(2,1)S(1)}, bf16[256,640]{1,0:T(8,128)(2,1)S(1)}, u32[]{:S(2)}, u32[]{:S(2)}) collective-permute-start(bf16[256,640]{1,0:T(8,128)(2,1)S(1)} %get-tuple-element.59), channel_id=1, source_target_pairs={{0,1},{1,0},{2,3},{3,2},{4,5},{5,4},{6,7},{7,6},{8,9},{9,8},{10,11... | collective-permute-start | bytes 983048 | tf_op jit(solution)/shard_map/ppermute | solution.py:30
  204.9 11.2 %collective-permute-start.42 = (bf16[256,640]{1,0:T(8,128)(2,1)S(1)}, bf16[256,640]{1,0:T(8,128)(2,1)S(1)}, u32[]{:S(2)}, u32[]{:S(2)}) collective-permute-start(bf16[256,640]{1,0:T(8,128)(2,1)S(1)} %get-tuple-element.53), channel_id=1, source_target_pairs={{0,3},{1,2},{2,1},{3,0},{4,7},{5,6},{6,5},{7,4},{8,11},{9,10},{10,... | collective-permute-start | bytes 983048 | tf_op jit(solution)/shard_map/ppermute | solution.py:30
  210.6 12.1 %collective-permute-start.45 = (bf16[256,768]{1,0:T(8,128)(2,1)S(1)}, bf16[256,768]{1,0:T(8,128)(2,1)S(1)}, u32[]{:S(2)}, u32[]{:S(2)}) collective-permute-start(bf16[256,768]{1,0:T(8,128)(2,1)S(1)} %get-tuple-element.57), channel_id=1, source_target_pairs={{0,4},{1,5},{2,6},{3,7},{4,0},{5,1},{6,2},{7,3},{8,12},{9,13},{10,... | collective-permute-start | bytes 1179656 | tf_op jit(solution)/shard_map/ppermute | solution.py:30
  214.7 9.4 %collective-permute-start.49 = (bf16[128,640]{1,0:T(8,128)(2,1)S(1)}, bf16[128,640]{1,0:T(8,128)(2,1)S(1)}, u32[]{:S(2)}, u32[]{:S(2)}) collective-permute-start(bf16[128,640]{1,0:T(8,128)(2,1)S(1)} %slice.275), channel_id=1, source_target_pairs={{0,3},{1,2},{2,1},{3,0},{4,7},{5,6},{6,5},{7,4},{8,11},{9,10},{10,... | collective-permute-start | bytes 491528 | tf_op jit(solution)/shard_map/ppermute | solution.py:30
  216.2 9.4 %collective-permute-start.43 = (bf16[128,640]{1,0:T(8,128)(2,1)S(1)}, bf16[128,640]{1,0:T(8,128)(2,1)S(1)}, u32[]{:S(2)}, u32[]{:S(2)}) collective-permute-start(bf16[128,640]{1,0:T(8,128)(2,1)S(1)} %slice.276), channel_id=1, source_target_pairs={{0,4},{1,5},{2,6},{3,7},{4,0},{5,1},{6,2},{7,3},{8,12},{9,13},{10,... | collective-permute-start | bytes 491528 | tf_op jit(solution)/shard_map/ppermute | solution.py:30
  (50 other events, 540.5 us)
